TPU v7x, 32 devices: a whole 2x2x4 slice. The times are simulated.
32 devices in a mesh: expert: 16 (over z, y, x), tensor: 2 (over core).
Axes of the slice: x: 2, y: 2, z: 4, core: 2. Of those that a mesh axis runs over, the one named last changes fastest.
Arguments:
- tokens: bfloat16 [36864, 768], P(('expert', 'tensor')), may hold values from -6 to 6
- gains: float32 [768], replicated, may hold values from 0.5 to 1.5
- shifts: float32 [768], replicated, may hold values from -1 to 1
- projection: bfloat16 [768, 2304], replicated, may hold values from -0.21875 to 0.21875
- mixing: bfloat16 [768, 768], replicated, may hold values from -0.875 to 0.875
- factors: float32 [768], replicated, may hold values from 0.5 to 1.5
- biases: float32 [768], replicated, may hold values from -1 to 1
- centroids: bfloat16 [4, 768], replicated, may hold values from -0.15625 to 0.15625
- expanding: bfloat16 [16, 768, 768], P('expert', None, 'tensor'), may hold values from -0.21875 to 0.21875
- contracting: bfloat16 [16, 768, 768], P('expert', 'tensor'), may hold values from -0.21875 to 0.21875
- routes: int32 [36864, 1], P(('expert', 'tensor')), may hold values from 0 to 3; in each aligned block of 1152 rows (0 to 1151, 1152 to 2303, ...) at most 576 rows name the same one
- lengths: int32 [32, 4], P(('expert', 'tensor')), may hold values from 1 to 1024, 1152 in all within a row
- cotangent: bfloat16 [36864, 768], P(('expert', 'tensor')), may hold values from -6 to 6
Outputs:
- layer_output: bfloat16 [36864, 768], P(('expert', 'tensor'))
- balance: float32 [], replicated
- grad_tokens: float32 [36864, 768], P(('expert', 'tensor'))
- grad_gains: float32 [768], replicated
- grad_shifts: float32 [768], replicated
- grad_projection: float32 [768, 2304], replicated
- grad_mixing: float32 [768, 768], replicated
- grad_factors: float32 [768], replicated
- grad_biases: float32 [768], replicated
- grad_centroids: float32 [4, 768], replicated
- grad_expanding: float32 [16, 768, 768], P('expert', None, 'tensor')
- grad_contracting: float32 [16, 768, 768], P('expert', 'tensor')
Inputs may be any that keep to these rules, and one draw needn't show every extreme that they name: `routes`: in each device's block of 1152 rows no expert is named more than 576 times, a bound that some block reaches. `lengths`: each row sums to 1152; its largest entry is 1024.
All inputs are finite; a program needn't handle non-finite values.
Results may differ from a plain program's by a relative error of at most 0.014.
Values may be sent and summed in bfloat16 or wider, within the bound.
A program may use at most 384 MiB of HBM per device.

v0:
```python
from functools import partial

import jax
import jax.numpy as jnp
from jax import lax
from jax.experimental import pallas as pl
from jax.experimental.pallas import tpu as pltpu
from jax.sharding import PartitionSpec as P

HEADS = 12


highest = lax.Precision.HIGHEST
epsilon = 1e-05


def running(values):
    places = jnp.arange(values.shape[0])
    return jnp.sum(jnp.where(places[:, None] >= places[None, :], values[None, :], 0), axis=1)


def earlier(picks):
    places = jnp.arange(picks.shape[0])
    before = (places[:, None] > places[None, :]).astype(jnp.bfloat16)
    return jnp.dot(
        before, picks.astype(jnp.bfloat16), preferred_element_type=jnp.float32
    ).astype(jnp.int32)


def norm_parts(values, gain, shift):
    centered = values - jnp.mean(values, axis=1, keepdims=True)
    scale = lax.rsqrt(jnp.mean(centered * centered, axis=1, keepdims=True) + epsilon)
    normal = centered * scale
    return (normal * gain + shift, normal, scale)


def norm_back(upstream, normal, scale, gain):
    scaled = upstream * gain
    inner = (
        scaled
        - jnp.mean(scaled, axis=1, keepdims=True)
        - normal * jnp.mean(scaled * normal, axis=1, keepdims=True)
    )
    return (inner * scale, jnp.sum(upstream * normal, axis=0), jnp.sum(upstream, axis=0))


def gelu_slope(values):
    return (
        0.5 * (1.0 + lax.erf(values * 0.7071067811865476))
        + values * jnp.exp(-0.5 * values * values) * 0.3989422804014327
    )


def expert_forward(gathered, upward, downward):
    before = jnp.dot(gathered, upward, preferred_element_type=jnp.float32)
    active = jax.nn.gelu(before, approximate=False).astype(jnp.bfloat16)
    return jnp.dot(active, downward, preferred_element_type=jnp.float32)


def expert_backward(gathered, incoming, upward, downward):
    before = jnp.dot(gathered, upward, preferred_element_type=jnp.float32)
    active = jax.nn.gelu(before, approximate=False).astype(jnp.bfloat16)
    down_grad = jnp.einsum("rf,rd->fd", active, incoming, preferred_element_type=jnp.float32)
    through = jnp.einsum("rd,fd->rf", incoming, downward, preferred_element_type=jnp.float32)
    hidden_grad = (through * gelu_slope(before)).astype(jnp.bfloat16)
    up_grad = jnp.einsum("rd,rf->df", gathered, hidden_grad, preferred_element_type=jnp.float32)
    return (up_grad, down_grad, hidden_grad)


def head_forward(allowed, item):
    query, keys, values = item
    factor = query.shape[1] ** (-0.5)
    scores = jnp.einsum("qd,kd->qk", query, keys, preferred_element_type=jnp.float32) * factor
    scores = jnp.where(allowed, scores, -1000000000.0)
    peak = jnp.max(scores, axis=1, keepdims=True)
    weights = jnp.exp(scores - peak)
    total = jnp.sum(weights, axis=1, keepdims=True)
    mixed = jnp.dot(
        (weights / total).astype(jnp.bfloat16), values, preferred_element_type=jnp.float32
    )
    return (mixed.astype(jnp.bfloat16), (peak + jnp.log(total))[:, 0])


def head_backward(allowed, item):
    query, keys, values, upstream, log_total = item
    factor = query.shape[1] ** (-0.5)
    scores = jnp.einsum("qd,kd->qk", query, keys, preferred_element_type=jnp.float32) * factor
    scores = jnp.where(allowed, scores, -1000000000.0)
    probs = jnp.exp(scores - log_total[:, None])
    value_grad = jnp.einsum(
        "qk,qd->kd", probs.astype(jnp.bfloat16), upstream, preferred_element_type=jnp.float32
    )
    prob_grad = jnp.einsum("qd,kd->qk", upstream, values, preferred_element_type=jnp.float32)
    inner = jnp.sum(prob_grad * probs, axis=1, keepdims=True)
    score_grad = (probs * (prob_grad - inner)).astype(jnp.bfloat16)
    query_grad = (
        jnp.einsum("qk,kd->qd", score_grad, keys, preferred_element_type=jnp.float32) * factor
    )
    key_grad = (
        jnp.einsum("qk,qd->kd", score_grad, query, preferred_element_type=jnp.float32) * factor
    )
    return (query_grad, key_grad, value_grad)


def moving_tokens(
    tokens,
    gains,
    shifts,
    projection,
    mixing,
    factors,
    biases,
    centroids,
    expanding,
    contracting,
    routes,
    lengths,
    cotangent,
):
    count, width = tokens.shape
    experts = centroids.shape[0]
    groups = lax.axis_size("expert")
    slab_count = groups // experts
    capacity = max(2, 2 * count // experts)
    total_tokens = count * groups * lax.axis_size("tensor")
    average = total_tokens / experts
    route = routes[:, 0]
    picks = route[:, None] == jnp.arange(experts, dtype=jnp.int32)[None, :]
    picks_int = picks.astype(jnp.int32)
    picks_float = picks.astype(jnp.float32)
    loads = lax.psum(jnp.sum(picks_float, axis=0), ("expert", "tensor"))
    spread = (loads - average) / average
    token_spread = jnp.sum(jnp.where(picks, spread[None, :], 0.0), axis=1)
    ranks = jnp.sum(earlier(picks) * picks_int, axis=1)
    slots = route * capacity + ranks
    places = jnp.arange(count, dtype=jnp.int32)
    documents = jnp.sum(
        (places[:, None] >= running(lengths[0])[None, :]).astype(jnp.int32), axis=1
    )
    allowed = (places[:, None] >= places[None, :]) & (documents[:, None] == documents[None, :])
    inputs = tokens.astype(jnp.float32)
    entry, entry_normal, entry_scale = norm_parts(inputs, gains, shifts)
    entry = entry.astype(jnp.bfloat16)
    joint = jnp.dot(entry, projection, preferred_element_type=jnp.float32).astype(jnp.bfloat16)
    heads = joint.reshape(count, 3, HEADS, width // HEADS).transpose(1, 2, 0, 3)
    mixed, log_total = lax.map(partial(head_forward, allowed), (heads[0], heads[1], heads[2]))
    mixed_rows = mixed.transpose(1, 0, 2).reshape(count, width)
    residual = inputs + jnp.dot(mixed_rows, mixing, preferred_element_type=jnp.float32)
    normed, mixer_normal, mixer_scale = norm_parts(residual, factors, biases)
    chosen = jnp.dot(picks.astype(jnp.bfloat16), centroids, preferred_element_type=jnp.float32)
    gates = jax.nn.sigmoid(jnp.sum(normed * chosen, axis=1))
    outgoing = (
        jnp.zeros((experts * capacity, width), jnp.bfloat16)
        .at[slots]
        .set(normed.astype(jnp.bfloat16))
    )
    copies = jnp.broadcast_to(
        outgoing.reshape(experts, 1, capacity, width), (experts, slab_count, capacity, width)
    ).reshape(groups, capacity, width)
    arrived = lax.all_to_all(copies, "expert", split_axis=0, concat_axis=0, tiled=True)
    sources = groups * capacity
    own_rows = arrived.reshape(sources, width)
    gathered = lax.all_gather(own_rows, "tensor", axis=0, tiled=True)
    produced = lax.psum_scatter(
        expert_forward(gathered, expanding[0], contracting[0]).astype(jnp.bfloat16),
        "tensor",
        scatter_dimension=0,
        tiled=True,
    )
    returned = lax.all_to_all(
        produced.reshape(arrived.shape), "expert", split_axis=0, concat_axis=0, tiled=True
    )
    combined = jnp.sum(
        returned.reshape(experts, slab_count, capacity, width).astype(jnp.float32), axis=1
    ).reshape(experts * capacity, width)
    picked = combined[slots]
    layer_output = (residual + gates[:, None] * picked).astype(jnp.bfloat16)
    balance_part = jnp.sum(token_spread * gates) / total_tokens
    upstream = cotangent.astype(jnp.float32)
    gate_grad = jnp.sum(upstream * picked, axis=1)
    logit_grad = (gate_grad + token_spread / total_tokens) * gates * (1.0 - gates)
    scaled_rows = (gates[:, None] * upstream).astype(jnp.bfloat16)
    grad_slots = jnp.zeros((experts * capacity, width), jnp.bfloat16).at[slots].set(scaled_rows)
    grad_copies = jnp.broadcast_to(
        grad_slots.reshape(experts, 1, capacity, width), (experts, slab_count, capacity, width)
    ).reshape(groups, capacity, width)
    incoming = lax.all_to_all(
        grad_copies, "expert", split_axis=0, concat_axis=0, tiled=True
    ).reshape(sources, width)
    incoming_pair = lax.all_gather(incoming, "tensor", axis=0, tiled=True)
    up_share, down_share, hidden_grad = expert_backward(
        gathered, incoming_pair, expanding[0], contracting[0]
    )
    back_rows = lax.psum_scatter(
        jnp.einsum(
            "rf,df->rd", hidden_grad, expanding[0], preferred_element_type=jnp.float32
        ).astype(jnp.bfloat16),
        "tensor",
        scatter_dimension=0,
        tiled=True,
    )
    back = lax.all_to_all(
        back_rows.reshape(arrived.shape), "expert", split_axis=0, concat_axis=0, tiled=True
    )
    back_sum = jnp.sum(
        back.reshape(experts, slab_count, capacity, width).astype(jnp.float32), axis=1
    ).reshape(experts * capacity, width)
    normed_grad = back_sum[slots] + logit_grad[:, None] * chosen
    centroid_grad = jnp.einsum(
        "te,td->ed", picks_float, logit_grad[:, None] * normed, precision=highest
    )
    mixer_back, factor_grad, bias_grad = norm_back(normed_grad, mixer_normal, mixer_scale, factors)
    residual_grad = upstream + mixer_back
    branch_grad = residual_grad.astype(jnp.bfloat16)
    mixing_grad = jnp.einsum(
        "td,te->de", mixed_rows, branch_grad, preferred_element_type=jnp.float32
    )
    mixed_grad = jnp.einsum(
        "te,de->td", branch_grad, mixing, preferred_element_type=jnp.float32
    ).astype(jnp.bfloat16)
    head_grads = mixed_grad.reshape(count, HEADS, width // HEADS).transpose(1, 0, 2)
    query_grad, key_grad, value_grad = lax.map(
        partial(head_backward, allowed), (heads[0], heads[1], heads[2], head_grads, log_total)
    )
    joint_grad = (
        jnp.stack((query_grad, key_grad, value_grad))
        .transpose(2, 0, 1, 3)
        .reshape(count, 3 * width)
        .astype(jnp.bfloat16)
    )
    projection_grad = jnp.einsum("td,te->de", entry, joint_grad, preferred_element_type=jnp.float32)
    entry_back = jnp.einsum("te,de->td", joint_grad, projection, preferred_element_type=jnp.float32)
    entry_input, gain_grad, shift_grad = norm_back(entry_back, entry_normal, entry_scale, gains)
    token_grad = residual_grad + entry_input
    summed = lax.psum(
        (
            gain_grad,
            shift_grad,
            projection_grad,
            mixing_grad,
            factor_grad,
            bias_grad,
            centroid_grad,
            balance_part,
        ),
        ("expert", "tensor"),
    )
    return (
        layer_output,
        summed[7],
        token_grad,
        summed[0],
        summed[1],
        summed[2],
        summed[3],
        summed[4],
        summed[5],
        summed[6],
        up_share[None],
        down_share[None],
    )


HALF_LOG = 1.4426950408889634
LN2 = 0.6931471805599453
NT = (((1,), (1,)), ((), ()))
TN = (((0,), (0,)), ((), ()))
VMEM_LIMIT = 60 * 1024 * 1024


def query_blocks(count):
    step = 256 if count > 256 else count
    return [(i, min(i + step, count)) for i in range(0, count, step)]


def document_starts(lengths_ref, places):
    starts = jnp.zeros_like(places)
    end = 0
    for d in range(lengths_ref.shape[0]):
        end = end + lengths_ref[d]
        starts = jnp.where(places >= end, end, starts)
    return starts


MESH = pl.DeviceIdType.MESH


def neighbours(slabs):
    me, core = lax.axis_index("expert"), lax.axis_index("tensor")
    plane = lax.div(me, slabs)
    x = lax.rem(me, 2)
    y = lax.rem(lax.div(me, 2), 2)
    return me, core, plane, (me + 1 - 2 * x, core), (me + 2 - 4 * y, core), (me, 1 - core)


def greet(partners):
    barrier = pltpu.get_barrier_semaphore()
    number = 0
    for device, there in partners:
        @pl.when(there)
        def _(device=device):
            pl.semaphore_signal(barrier, inc=1, device_id=device, device_id_type=MESH)
        number = number + there.astype(jnp.int32)
    pl.semaphore_wait(barrier, number)


def score_bias(bias_ref, lengths_ref, count):
    places = lax.broadcasted_iota(jnp.int32, (1, count), 1)
    starts = document_starts(lengths_ref, places)
    for s, e in query_blocks(count):
        row = lax.broadcasted_iota(jnp.int32, (e - s, count), 0) + s
        seen = (row <= places) & (row >= starts)
        bias_ref[s:e, :] = jnp.where(seen, 0.0, -1e9)


def row_norm(values, gain, shift):
    centered = values - jnp.mean(values, axis=1, keepdims=True)
    scale = lax.rsqrt(jnp.mean(centered * centered, axis=1, keepdims=True) + epsilon)
    normal = centered * scale
    return normal * gain + shift, normal, scale


def chosen_rows(route, centroids_ref, experts):
    chosen = jnp.zeros((route.shape[0], centroids_ref.shape[1]), jnp.float32)
    for e in range(experts):
        chosen = jnp.where(route == e, centroids_ref[e : e + 1, :].astype(jnp.float32), chosen)
    return chosen


def front_kernel(
    planes,
    slabs,
    lengths_ref,
    tokens_ref,
    norms_ref,
    projection_ref,
    mixing_ref,
    centroids_ref,
    route_row_ref,
    route_ref,
    cot_ref,
    up_ref,
    down_ref,
    flipped_ref,
    joint_ref,
    mixed_ref,
    logs_ref,
    residual_ref,
    place_ref,
    loads_ref,
    sent_all,
    cot_all,
    gate_all,
    up_near,
    up_far,
    down_near,
    down_far,
    bias_ref,
    order_ref,
    normed_ref,
    entry_ref,
    sent_own,
    cot_own,
    gate_own,
    tally_ref,
    send_sem,
    recv_sem,
    local_sem,
):
    count, width = tokens_ref.shape
    experts = planes
    rows = sent_own.shape[0]
    half_rows = rows // 2
    pairs = width // 128
    factor = (width // HEADS) ** (-0.5) * HALF_LOG
    middle = planes - 1
    me, core, plane, beside_x, beside_y, beside_core = neighbours(slabs)
    hop_two = lax.rem(plane + 2, planes)
    hop_one = plane + 1 - 2 * lax.rem(plane, 2)
    here = lax.rem(me, slabs)
    always = plane >= 0
    greet(
        [
            (beside_x, always),
            (beside_y, always),
            (beside_core, always),
            ((hop_two * slabs + here, core), always),
            ((me + slabs, core), plane < planes - 1),
            ((me - slabs, core), plane > 0),
        ]
    )

    def remote(i, src, dst, device):
        return pltpu.make_async_remote_copy(
            src_ref=src, dst_ref=dst, send_sem=send_sem.at[i], recv_sem=recv_sem.at[i], device_id=device, device_id_type=MESH
        )

    owns, nears, fars = (up_ref, down_ref), (up_near, down_near), (up_far, down_far)
    stride = 2 * (planes - 1) + 2 * planes - 1

    def hop(kind, sign, r):
        src = owns[kind].at[0] if r == 1 else nears[kind].at[middle - sign * (r - 1)]
        i = kind * stride + (r - 1) * 2 + (sign > 0)
        return remote(i, src, nears[kind].at[middle - sign * r], (me + sign * slabs, core))

    def hop_sent(sign, r):
        ahead = plane if sign > 0 else planes - 1 - plane
        return (ahead >= r - 1) & (ahead < planes - 1)

    def hop_came(sign, r):
        ahead = plane if sign > 0 else planes - 1 - plane
        return ahead >= r

    def aside(kind, slot):
        src = owns[kind].at[0] if slot == middle else nears[kind].at[slot]
        i = kind * stride + 2 * (planes - 1) + slot
        return remote(i, src, fars[kind].at[slot], beside_x)

    def held(slot):
        at = plane + slot - middle
        return (at >= 0) & (at < planes)

    def own_weights(kind):
        return pltpu.make_async_copy(owns[kind].at[0], nears[kind].at[middle], local_sem.at[kind])

    for kind in range(2):
        for sign in (1, -1):
            @pl.when(hop_sent(sign, 1))
            def _(kind=kind, sign=sign):
                hop(kind, sign, 1).start()
        aside(kind, middle).start()
        own_weights(kind).start()

    def forward_weights(kind, r):
        for sign in (1, -1):
            slot = middle - sign * r

            @pl.when(hop_came(sign, r))
            def _(sign=sign, slot=slot):
                hop(kind, sign, r).wait_recv()
                aside(kind, slot).start()

            if r < planes - 1:
                @pl.when(hop_sent(sign, r + 1))
                def _(sign=sign):
                    hop(kind, sign, r + 1).start()

    base = 2 * stride

    def row_copy(which, part, piece):
        own, everyone = ((cot_own, cot_all), (sent_own, sent_all))[which]
        at = pl.ds(piece * half_rows, half_rows)
        i = base + which * 6 + part * 2 + piece
        if part == 0:
            return remote(i, own.at[at], everyone.at[2, at], beside_y)
        if part == 1:
            return remote(i, own.at[at], everyone.at[1, at], beside_core)
        return remote(i, everyone.at[2, at], everyone.at[3, at], beside_core)

    def gate_copy(part):
        i = base + 12 + part
        if part == 0:
            return remote(i, gate_own, gate_all.at[2], beside_y)
        if part == 1:
            return remote(i, gate_own, gate_all.at[1], beside_core)
        return remote(i, gate_all.at[2], gate_all.at[3], beside_core)

    def own_rows(which):
        source, everyone = ((cot_own, cot_all), (sent_own, sent_all), (gate_own, gate_all))[which]
        return pltpu.make_async_copy(source, everyone.at[0], local_sem.at[2 + which])

    rounds = [beside_core, beside_x, beside_y, (hop_one * slabs + here, core), (hop_two * slabs + here, core)]

    def tally(k):
        return remote(base + 15 + k, tally_ref.at[2 * k], tally_ref.at[2 * k + 1], rounds[k])

    def tally_step(k):
        tally(k).wait_recv()
        total = tally_ref[2 * k] + tally_ref[2 * k + 1]
        if k + 1 < len(rounds):
            tally_ref[2 * k + 2] = total
            tally(k + 1).start()
        else:
            loads_ref[...] = total

    number = lax.broadcasted_iota(jnp.int32, (8, count), 0)
    picks = jnp.where(number == route_row_ref[...], 1.0, 0.0)
    chunk = 128
    for s in range(0, count, chunk):
        row = lax.broadcasted_iota(jnp.int32, (chunk, count), 0) + s
        column = lax.broadcasted_iota(jnp.int32, (chunk, count), 1)
        order_ref[s : s + chunk, :] = jnp.where(row < column, 1.0, 0.0).astype(jnp.bfloat16)
    ranks = jnp.dot(picks.astype(jnp.bfloat16), order_ref[0:count, :], preferred_element_type=jnp.float32)
    counts = jnp.sum(picks, axis=1, keepdims=True)
    padded = jnp.ceil(counts * (1.0 / ALIGN)) * ALIGN
    place = jnp.zeros((1, count), jnp.float32)
    start = jnp.zeros((1, 1), jnp.float32)
    for e in range(experts):
        place = place + picks[e : e + 1, :] * (ranks[e : e + 1, :] + start)
        start = start + padded[e : e + 1, :]
    place_ref[...] = jnp.broadcast_to(place, (8, count))
    tally_ref[0] = jnp.broadcast_to(counts, (8, 128))
    tally(0).start()
    for s in range(0, rows, 64):
        row = lax.broadcasted_iota(jnp.int32, (64, count), 0) + s
        order_ref[s : s + 64, :] = jnp.where(row.astype(jnp.float32) == place, 1.0, 0.0).astype(jnp.bfloat16)

    def sort_rows(source_ref, to_ref, which):
        for piece in range(2):
            at = slice(piece * half_rows, (piece + 1) * half_rows)
            to_ref[at, :] = jnp.dot(
                order_ref[at, :], source_ref[...], preferred_element_type=jnp.float32
            ).astype(jnp.bfloat16)
            row_copy(which, 0, piece).start()
            row_copy(which, 1, piece).start()

    sort_rows(cot_ref, cot_own, 0)
    own_rows(0).start()

    def project(i, _):
        at = pl.ds(pl.multiple_of(i * 192, 192), 192)
        entry, _, _ = row_norm(tokens_ref[at, :].astype(jnp.float32), norms_ref[0:1, :], norms_ref[1:2, :])
        entry = entry.astype(jnp.bfloat16)
        entry_ref[at, :] = entry
        joint_ref[at, :] = jnp.dot(entry, projection_ref[...], preferred_element_type=jnp.float32).astype(jnp.bfloat16)
        return 0

    lax.fori_loop(0, count // 192, project, 0)
    score_bias(bias_ref, lengths_ref, count)
    forward_weights(0, 1)
    tally_step(0)

    first = lax.broadcasted_iota(jnp.int32, (1, 128), 1) < 64

    def attend(p, _):
        lanes = pl.ds(pl.multiple_of(p * 128, 128), 128)
        keys = pl.ds(pl.multiple_of(width + p * 128, 128), 128)
        values = pl.ds(pl.multiple_of(2 * width + p * 128, 128), 128)
        for s, e in query_blocks(count):
            outs = []
            for half in range(2):
                q = jnp.where(first == (half == 0), joint_ref[s:e, lanes], jnp.bfloat16(0))
                scores = lax.dot_general(joint_ref[0:e, keys], q, NT, preferred_element_type=jnp.float32)
                scores = scores * factor + bias_ref[0:e, s:e]
                peak = jnp.max(scores, axis=0, keepdims=True)
                weights = jnp.exp2(scores - peak)
                total = jnp.sum(weights, axis=0, keepdims=True)
                probs = (weights * (1.0 / total)).astype(jnp.bfloat16)
                outs.append(
                    lax.dot_general(probs, joint_ref[0:e, values], TN, preferred_element_type=jnp.float32)
                )
                logs_ref[p, half : half + 1, s:e] = peak + jnp.log2(total)
            mixed_ref[s:e, lanes] = jnp.where(first, outs[0], outs[1]).astype(jnp.bfloat16)

        @pl.when(p == 2)
        def _():
            forward_weights(1, 1)
            tally_step(1)

        @pl.when(p == 4)
        def _():
            forward_weights(0, 2)
            tally_step(2)

        return 0

    lax.fori_loop(0, pairs, attend, 0)

    lane = lax.broadcasted_iota(jnp.int32, (1, 128), 1)

    def mix(i, _):
        at = pl.ds(pl.multiple_of(i * 192, 192), 192)
        residual = tokens_ref[at, :].astype(jnp.float32) + jnp.dot(
            mixed_ref[at, :], mixing_ref[...], preferred_element_type=jnp.float32
        )
        residual_ref[at, :] = residual
        normed, _, _ = row_norm(residual, norms_ref[2:3, :], norms_ref[3:4, :])
        chosen = chosen_rows(route_ref[at, :], centroids_ref, experts)
        gate = 1.0 / (1.0 + jnp.exp(-jnp.sum(normed * chosen, axis=1, keepdims=True)))
        high = gate.astype(jnp.bfloat16).astype(jnp.float32)
        mid = (gate - high).astype(jnp.bfloat16).astype(jnp.float32)
        low = gate - high - mid
        parts = jnp.where(lane == 0, high, jnp.where(lane == 1, mid, jnp.where(lane == 2, low, 0.0)))
        normed_ref[at, 0:width] = normed.astype(jnp.bfloat16)
        normed_ref[at, width : width + 128] = parts.astype(jnp.bfloat16)
        return 0

    lax.fori_loop(0, count // 192, mix, 0)
    for piece in range(2):
        at = slice(piece * half_rows, (piece + 1) * half_rows)
        moved = jnp.dot(order_ref[at, :], normed_ref[...], preferred_element_type=jnp.float32)
        sent_own[at, :] = moved[:, 0:width].astype(jnp.bfloat16)
        row_copy(1, 0, piece).start()
        row_copy(1, 1, piece).start()
        bias_ref[at, 0:128] = jnp.broadcast_to(
            jnp.sum(moved[:, width : width + 128], axis=1, keepdims=True), (half_rows, 128)
        )
    forward_weights(1, 2)
    tally_step(3)
    for piece in range(2):
        row_copy(0, 0, piece).wait_recv()
        row_copy(0, 2, piece).start()
    gates = jnp.transpose(bias_ref[0:rows, 0:128])
    gate_own[0:1, :] = gates[0:1, :]
    gate_own[1:2, :] = jnp.zeros((1, rows), jnp.float32)
    for e in range(8):
        gate_own[1:2, e : e + 1] = padded[e : e + 1, :]
    gate_copy(0).start()
    gate_copy(1).start()
    own_rows(1).start()
    own_rows(2).start()
    for s in range(0, count, 384):
        flipped_ref[:, s : s + 384] = jnp.transpose(entry_ref[s : s + 384, :])

    for kind in range(2):
        forward_weights(kind, 3)
    gate_copy(0).wait_recv()
    gate_copy(2).start()
    tally_step(4)
    for piece in range(2):
        row_copy(1, 0, piece).wait_recv()
        row_copy(1, 2, piece).start()

    for which in range(2):
        for part in range(3):
            for piece in range(2):
                copy = row_copy(which, part, piece)
                copy.wait_send()
                if part:
                    copy.wait_recv()
    for part in range(3):
        gate_copy(part).wait_send()
        if part:
            gate_copy(part).wait_recv()
    for k in range(len(rounds)):
        tally(k).wait_send()
    for which in range(3):
        own_rows(which).wait()
    for kind in range(2):
        own_weights(kind).wait()
        for r in range(1, planes):
            for sign in (1, -1):
                @pl.when(hop_sent(sign, r))
                def _(kind=kind, sign=sign, r=r):
                    hop(kind, sign, r).wait_send()
        for slot in range(2 * planes - 1):
            @pl.when(held(slot))
            def _(kind=kind, slot=slot):
                aside(kind, slot).wait()


def front_stage(
    tokens, norms, projection, mixing, centroids, expanding, contracting, route, lengths, cotangent, planes, slabs
):
    count, width = tokens.shape
    rows = aligned_rows(count, planes)
    pairs = width // 128
    slots = 2 * planes - 1
    bf16, f32 = jnp.bfloat16, jnp.float32
    shape = jax.ShapeDtypeStruct
    anywhere = pl.BlockSpec(memory_space=pl.ANY)
    local = pl.BlockSpec(memory_space=pltpu.VMEM)
    dma = pltpu.SemaphoreType.DMA
    copies = 2 * (2 * (planes - 1) + slots) + 12 + 3 + 5
    outs = [
        (shape((width, count), bf16), local),
        (shape((count, 3 * width), bf16), local),
        (shape((count, width), bf16), local),
        (shape((pairs, 2, count), f32), local),
        (shape((count, width), f32), local),
        (shape((8, count), f32), local),
        (shape((8, 128), f32), local),
        (shape((4, rows, width), bf16), anywhere),
        (shape((4, rows, width), bf16), anywhere),
        (shape((4, 8, rows), f32), anywhere),
        (shape((slots,) + expanding.shape[1:], bf16), anywhere),
        (shape((slots,) + expanding.shape[1:], bf16), anywhere),
        (shape((slots,) + contracting.shape[1:], bf16), anywhere),
        (shape((slots,) + contracting.shape[1:], bf16), anywhere),
    ]
    return pl.pallas_call(
        partial(front_kernel, planes, slabs),
        out_shape=[o[0] for o in outs],
        in_specs=[pl.BlockSpec(memory_space=pltpu.SMEM)] + [local] * 8 + [anywhere] * 2,
        out_specs=[o[1] for o in outs],
        scratch_shapes=[
            pltpu.VMEM((rows, count), f32),
            pltpu.VMEM((rows, count), bf16),
            pltpu.VMEM((count, width + 128), bf16),
            pltpu.VMEM((count, width), bf16),
            pltpu.VMEM((rows, width), bf16),
            pltpu.VMEM((rows, width), bf16),
            pltpu.VMEM((8, rows), f32),
            pltpu.VMEM((10, 8, 128), f32),
            dma((copies,)),
            dma((copies,)),
            dma((5,)),
        ],
        compiler_params=pltpu.CompilerParams(
            collective_id=0, has_side_effects=True, vmem_limit_bytes=VMEM_LIMIT
        ),
    )(
        lengths[0],
        tokens,
        norms,
        projection,
        mixing,
        centroids,
        route.reshape(1, -1),
        route,
        cotangent,
        expanding,
        contracting,
    )


STEP = 192


def rear_kernel(
    planes,
    slabs,
    total_tokens,
    lengths_ref,
    tokens_ref,
    norms_ref,
    projection_ref,
    mixing_ref,
    centroids_ref,
    route_ref,
    cot_ref,
    flipped_ref,
    joint_in,
    mixed_ref,
    logs_ref,
    residual_in,
    place_ref,
    loads_ref,
    dots_ref,
    back_all,
    made_all,
    near_all,
    far_all,
    layer_ref,
    token_ref,
    vector_ref,
    up_out,
    down_out,
    shared_out,
    core_land,
    y_land,
    x_land,
    z_land,
    joint_ref,
    residual_ref,
    bias_ref,
    upstream_ref,
    a_ref,
    b_ref,
    place_col,
    gate_col,
    dot_land,
    part_ref,
    stage_ref,
    own_ref,
    own_core,
    own_first,
    own_second,
    own_z,
    piece_ref,
    tally_ref,
    key_sums,
    send_sem,
    recv_sem,
    local_sem,
):
    count, width = tokens_ref.shape
    experts = planes
    rows = a_ref.shape[0]
    half_rows = rows // 2
    pairs = width // 128
    half = width // 2
    scale = (width // HEADS) ** (-0.5)
    factor = scale * HALF_LOG
    average = total_tokens / experts
    me, core, plane, beside_x, beside_y, beside_core = neighbours(slabs)
    x = lax.rem(me, 2)
    y = lax.rem(lax.div(me, 2), 2)
    here = lax.rem(me, slabs)
    diagonal = (beside_y[0], 1 - core)
    always = plane >= 0
    others = [(lax.rem(plane + d, planes) * slabs + here, core) for d in range(1, planes)]
    greet([(d, always) for d in [beside_x, beside_y, beside_core, diagonal] + others])
    ids = {}

    def remote(key, src, dst, device):
        i = ids.setdefault(key, len(ids))
        return pltpu.make_async_remote_copy(
            src_ref=src, dst_ref=dst, send_sem=send_sem.at[i], recv_sem=recv_sem.at[i], device_id=device, device_id_type=MESH
        )

    def fetch(i, src, dst):
        return pltpu.make_async_copy(src, dst, local_sem.at[i])

    loads = [fetch(0, joint_in, joint_ref), fetch(1, residual_in, residual_ref)]
    for copy in loads:
        copy.start()

    alls = (back_all, made_all)

    def to_core(which, second, piece):
        at = pl.ds(piece * half_rows, half_rows)
        return remote(
            ("core", which, second, piece), alls[which].at[1 + 2 * second, at], core_land.at[which, second, at], beside_core
        )

    def to_y(which, piece):
        size = half_rows // (1 + which)
        at = pl.ds(piece * size, size)
        return remote(("y", which, piece), a_ref.at[at], y_land.at[which, at], beside_y)

    def dot_copy(k):
        return remote(("dot", k), dots_ref.at[1 + k], dot_land.at[k], (beside_core, beside_y, diagonal)[k])

    for which in range(2):
        for second in (1, 0):
            for piece in range(2):
                to_core(which, second, piece).start()
        if which == 0:
            for k in range(3):
                dot_copy(k).start()

    def target(sign, r):
        e = plane + sign * r
        return jnp.clip(e, 0, planes - 1), (e >= 0) & (e < planes)

    def share_x(sign, r):
        e, _ = target(sign, r)
        return remote(("x", sign, r), far_all.at[e], x_land.at[e], beside_x)

    def share_z(sign, r):
        return remote(
            ("z", sign, r),
            stage_ref.at[0 if sign > 0 else 1],
            z_land.at[0 if sign > 0 else 1, r - 1],
            (jnp.clip(me + sign * slabs, 0, planes * slabs - 1), core),
        )

    ways = [(s, r) for r in range(planes - 1, 0, -1) for s in (1, -1)] + [(1, 0)]
    def start_shares(distance):
        for sign, r in ways:
            if r == distance:
                @pl.when(target(sign, r)[1])
                def _(sign=sign, r=r):
                    share_x(sign, r).start()

    for distance in range(planes - 1, 1, -1):
        start_shares(distance)

    def add_pieces(into, sources, size, step):
        def one(i, _):
            at = pl.ds(pl.multiple_of(i * step, step), step)
            total = sources[0][at, :].astype(jnp.float32)
            for s in sources[1:]:
                total = total + s[at, :].astype(jnp.float32)
            into[at, :] = total.astype(into.dtype)
            return 0
        lax.fori_loop(0, size // step, one, 0)

    def share_step(sign, r):
        e, valid = target(sign, r)
        lane = 0 if sign > 0 else 1

        @pl.when(valid)
        def _():
            first = fetch(2, near_all.at[e], part_ref.at[0])
            first.start()
            share_x(sign, r).wait_recv()
            second = fetch(3, x_land.at[e], part_ref.at[1])
            second.start()
            if r < planes - 1:
                @pl.when(target(sign, r + 1)[1])
                def _():
                    share_z(sign, r + 1).wait_send()
            first.wait()
            second.wait()
            add_pieces(stage_ref.at[lane], [part_ref.at[0], part_ref.at[1]], part_ref.shape[1], 96)
            if r < planes - 1:
                @pl.when((plane - sign >= 0) & (plane - sign < planes))
                def _():
                    share_z(sign, r + 1).wait_recv()
                    third = fetch(2, z_land.at[lane, r], part_ref.at[0])
                    third.start()
                    third.wait()
                    add_pieces(stage_ref.at[lane], [stage_ref.at[lane], part_ref.at[0]], part_ref.shape[1], 96)
            share_z(sign, r).start()

    def share_end():
        share_x(1, 0).wait_recv()
        copies = [fetch(2, near_all.at[plane], part_ref.at[0]), fetch(3, x_land.at[plane], part_ref.at[1])]
        for copy in copies:
            copy.start()
        for copy in copies:
            copy.wait()

        def put(sources, more):
            def rows_of(i, _):
                at = pl.ds(pl.multiple_of(i * 96, 96), 96)
                total = sources[0][at, :].astype(jnp.float32)
                if len(sources) > 1:
                    total = total + sources[1][at, :].astype(jnp.float32)
                up_out[at, :] = up_out[at, :] + total if more else total
                return 0
            lax.fori_loop(0, width // 96, rows_of, 0)

            def columns_of(i, _):
                at = pl.ds(pl.multiple_of(i * 96, 96), 96)
                for part in range(2):
                    source_at = pl.ds(pl.multiple_of(width + part * half + i * 96, 32), 96)
                    total = sources[0][source_at, :].astype(jnp.float32)
                    if len(sources) > 1:
                        total = total + sources[1][source_at, :].astype(jnp.float32)
                    to = slice(part * half, (part + 1) * half)
                    down_out[at, to] = down_out[at, to] + total if more else total
                return 0
            lax.fori_loop(0, half // 96, columns_of, 0)

        put([part_ref.at[0], part_ref.at[1]], False)
        for sign in (1, -1):
            lane = 0 if sign > 0 else 1

            @pl.when((plane - sign >= 0) & (plane - sign < planes))
            def _(sign=sign, lane=lane):
                share_z(sign, 1).wait_recv()
                third = fetch(2, z_land.at[lane, 0], part_ref.at[0])
                third.start()
                third.wait()
                put([part_ref.at[0]], True)

    q1, q2, q3, q4 = width // 2, width // 4, width // 8, width // 16
    base1 = core * q1
    base2 = base1 + y * q2
    base3 = base2 + x * q3

    def spot(start, size):
        return pl.ds(pl.multiple_of(start, 16), size)

    def corner(p):
        return lax.div(p, 2) * q4, pl.multiple_of(lax.rem(p, 2) * half, 128)

    def sum_copy(c, stage, d=0):
        own = own_ref.at[c % 3]
        if stage == "core":
            return remote((c, stage), own.at[spot((1 - core) * q1, q1)], own_core.at[c], beside_core)
        if stage == "first":
            return remote((c, stage), own.at[spot(base1 + (1 - y) * q2, q2)], own_first.at[c], beside_y)
        if stage == "second":
            return remote((c, stage), own.at[spot(base2 + (1 - x) * q3, q3)], own_second.at[c], beside_x)
        if stage == "z":
            r, k = corner(lax.rem(plane + d, planes))
            return remote(
                (c, stage, d), own.at[spot(base3 + r, q4), pl.ds(k, half)], own_z.at[c, d - 1], others[d - 1]
            )
        out = shared_out.at[c]
        if stage == "zz":
            r, k = corner(plane)
            return remote(
                (c, stage, d), piece_ref.at[c], out.at[spot(base3 + r, q4), pl.ds(k, half)], others[d - 1]
            )
        if stage == "second back":
            at = spot(base3, q3)
            return remote((c, stage), out.at[at], out.at[at], beside_x)
        if stage == "first back":
            at = spot(base2, q2)
            return remote((c, stage), out.at[at], out.at[at], beside_y)
        at = spot(base1, q1)
        return remote((c, stage), out.at[at], out.at[at], beside_core)

    def add_rows(c, start, size, came, step):
        def one(i, _):
            at = pl.ds(pl.multiple_of(i * step, step), step)
            mine = spot(start + i * step, step)
            own_ref[c % 3, mine, :] = (
                own_ref[c % 3, mine, :].astype(jnp.float32) + came[c, at, :].astype(jnp.float32)
            ).astype(jnp.bfloat16)
            return 0
        lax.fori_loop(0, size // step, one, 0)

    def keep_piece(c):
        r, k = corner(plane)
        return fetch(4 + c, piece_ref.at[c], shared_out.at[c, spot(base3 + r, q4), pl.ds(k, half)])

    def sum_step(c, stage):
        if stage == 0:
            sum_copy(c, "core").start()
        elif stage == 1:
            sum_copy(c, "core").wait_recv()
            add_rows(c, base1, q1, own_core, 48)
            sum_copy(c, "first").start()
        elif stage == 2:
            sum_copy(c, "first").wait_recv()
            add_rows(c, base2, q2, own_first, 48)
            sum_copy(c, "second").start()
        elif stage == 3:
            sum_copy(c, "second").wait_recv()
            add_rows(c, base3, q3, own_second, 48)
            for d in range(1, planes):
                sum_copy(c, "z", d).start()
        elif stage == 4:
            r, k = corner(plane)
            total = own_ref[c % 3, spot(base3 + r, q4), pl.ds(k, half)].astype(jnp.float32)
            for d in range(1, planes):
                sum_copy(c, "z", d).wait_recv()
                total = total + own_z[c, d - 1].astype(jnp.float32)
            piece_ref[c] = total.astype(jnp.bfloat16)
            keep_piece(c).start()
            for d in range(1, planes):
                sum_copy(c, "zz", d).start()
        elif stage == 5:
            keep_piece(c).wait()
            for d in range(1, planes):
                sum_copy(c, "zz", d).wait_recv()
            sum_copy(c, "second back").start()
        elif stage == 6:
            sum_copy(c, "second back").wait_recv()
            sum_copy(c, "first back").start()
        elif stage == 7:
            sum_copy(c, "first back").wait_recv()
            sum_copy(c, "cc").start()
        else:
            sum_copy(c, "cc").wait_recv()

    def sum_sent(c):
        for stage in ("core", "first", "second"):
            sum_copy(c, stage).wait_send()
        for d in range(1, planes):
            sum_copy(c, "z", d).wait_send()

    def sum_for_y(which):
        for piece in range(2):
            at = pl.ds(piece * half_rows, half_rows)
            first = fetch(2, alls[which].at[2, at], a_ref.at[at])
            first.start()
            to_core(which, 1, piece).wait_recv()
            second = fetch(3, core_land.at[which, 1, at], b_ref.at[at])
            second.start()
            first.wait()
            second.wait()
            add_pieces(a_ref.at[at], [a_ref.at[at], b_ref.at[at]], half_rows, 32)
            if which == 0:
                to_y(which, piece).start()

    sum_for_y(0)
    place_col[...] = jnp.transpose(place_ref[...])
    score_bias(bias_ref, lengths_ref, count)
    for copy in loads:
        copy.wait()
    vector_ref[...] = jnp.zeros_like(vector_ref)
    number = lax.broadcasted_iota(jnp.int32, (1, rows), 1).astype(jnp.float32)

    def order_of(at):
        return jnp.where(place_col[at, 0:1] == number, 1.0, 0.0)

    def chunk_of(i):
        return pl.ds(pl.multiple_of(i * STEP, STEP), STEP)

    steps = count // STEP

    def unsort(buffer, act):
        def one(i, _):
            at = chunk_of(i)
            act(at, jnp.dot(order_of(at).astype(jnp.bfloat16), buffer[...], preferred_element_type=jnp.float32))
            return 0
        lax.fori_loop(0, steps, one, 0)

    def set_token(at, value):
        token_ref[at, :] = value

    def add_token(at, value):
        token_ref[at, :] += value

    own_back = fetch(2, back_all.at[0], b_ref)
    own_back.start()
    own_back.wait()
    unsort(b_ref, set_token)
    for piece in range(2):
        to_core(0, 0, piece).wait_recv()
    core_back = fetch(2, core_land.at[0, 0], b_ref)
    core_back.start()
    core_back.wait()
    unsort(b_ref, add_token)
    for sign in (1, -1):
        share_step(sign, planes - 1)
    start_shares(1)
    for piece in range(2):
        to_y(0, piece).wait_recv()
    y_back = fetch(2, y_land.at[0], b_ref)
    y_back.start()
    y_back.wait()
    unsort(b_ref, add_token)
    for k in range(3):
        dot_copy(k).wait_recv()
    dots = dots_ref[0] + dot_land[0] + dot_land[1] + dot_land[2]
    dots = dots[0:1, :]

    def norm_step(i, _):
        at = chunk_of(i)
        normed, normal, spread_by = row_norm(residual_ref[at, :], norms_ref[2:3, :], norms_ref[3:4, :])
        route = route_ref[at, :]
        chosen = chosen_rows(route, centroids_ref, experts)
        gate = 1.0 / (1.0 + jnp.exp(-jnp.sum(normed * chosen, axis=1, keepdims=True)))
        gate_col[at, :] = jnp.broadcast_to(gate, (STEP, 128))
        gate_grad = jnp.sum(order_of(at) * dots, axis=1, keepdims=True)
        spread = jnp.zeros((STEP, 1), jnp.float32)
        for e in range(experts):
            spread = jnp.where(route == e, (loads_ref[e : e + 1, 0:1] - average) * (1.0 / average), spread)
        logit = (gate_grad + spread * (1.0 / total_tokens)) * gate * (1.0 - gate)
        above = token_ref[at, :] + logit * chosen
        pull = logit * normed
        vector_ref[2:3, :] += jnp.sum(above * normal, axis=0, keepdims=True)
        vector_ref[3:4, :] += jnp.sum(above, axis=0, keepdims=True)
        for e in range(experts):
            vector_ref[8 + e : 9 + e, :] += jnp.sum(jnp.where(route == e, pull, 0.0), axis=0, keepdims=True)
        vector_ref[4:5, :] += jnp.broadcast_to(
            jnp.sum(spread * gate, axis=0, keepdims=True) * (1.0 / total_tokens), (1, width)
        )
        scaled = above * norms_ref[2:3, :]
        inner = (
            scaled
            - jnp.mean(scaled, axis=1, keepdims=True)
            - normal * jnp.mean(scaled * normal, axis=1, keepdims=True)
        )
        grad = cot_ref[at, :].astype(jnp.float32) + inner * spread_by
        token_ref[at, :] = grad
        branch = grad.astype(jnp.bfloat16)
        layer_ref[at, :] = branch
        upstream_ref[at, :] = lax.dot_general(
            branch, mixing_ref[...], NT, preferred_element_type=jnp.float32
        ).astype(jnp.bfloat16)
        return 0

    lax.fori_loop(0, steps, norm_step, 0)
    own_ref[0] = lax.dot_general(
        mixed_ref[...], layer_ref[...], TN, preferred_element_type=jnp.float32
    ).astype(jnp.bfloat16)
    sum_step(0, 0)
    for piece in range(2):
        to_y(0, piece).wait_send()
    sum_for_y(1)
    for piece in range(2):
        to_y(1, piece).start()
    for sign in (1, -1):
        share_step(sign, planes - 2)

    first = lax.broadcasted_iota(jnp.int32, (1, 128), 1) < 64

    def attend(p, _):
        lanes = pl.ds(pl.multiple_of(p * 128, 128), 128)
        keys = pl.ds(pl.multiple_of(width + p * 128, 128), 128)
        values = pl.ds(pl.multiple_of(2 * width + p * 128, 128), 128)
        key_sum, value_sum = key_sums.at[0], key_sums.at[1]
        key_sum[...] = jnp.zeros_like(key_sum)
        value_sum[...] = jnp.zeros_like(value_sum)
        for s, e in query_blocks(count):
            both = jnp.transpose(
                upstream_ref[s:e, lanes].astype(jnp.float32) * mixed_ref[s:e, lanes].astype(jnp.float32)
            )
            found = []
            for h in range(2):
                mine = first == (h == 0)
                inner = jnp.sum(both[64 * h : 64 * h + 64, :], axis=0, keepdims=True)
                q = jnp.where(mine, joint_ref[s:e, lanes], jnp.bfloat16(0))
                u = jnp.where(mine, upstream_ref[s:e, lanes], jnp.bfloat16(0))
                scores = lax.dot_general(joint_ref[0:e, keys], q, NT, preferred_element_type=jnp.float32)
                probs = jnp.exp2(scores * factor + bias_ref[0:e, s:e] - logs_ref[p, h : h + 1, s:e])
                prob_grad = lax.dot_general(joint_ref[0:e, values], u, NT, preferred_element_type=jnp.float32)
                score_grad = (probs * (prob_grad - inner)).astype(jnp.bfloat16)
                value_sum[0:e, :] += jnp.dot(probs.astype(jnp.bfloat16), u, preferred_element_type=jnp.float32)
                key_sum[0:e, :] += jnp.dot(score_grad, q, preferred_element_type=jnp.float32)
                found.append(
                    lax.dot_general(score_grad, joint_ref[0:e, keys], TN, preferred_element_type=jnp.float32)
                )
            joint_ref[s:e, lanes] = (jnp.where(first, found[0], found[1]) * scale).astype(jnp.bfloat16)
        joint_ref[:, keys] = (key_sum[...] * scale).astype(jnp.bfloat16)
        joint_ref[:, values] = value_sum[...].astype(jnp.bfloat16)

        events = {
            0: [(0, 1)],
            2: [(0, 2), (1, 1)],
            3: [(0, 3)],
            4: [(0, 4), (1, 2), (2, 1)],
            5: [(0, 5), (1, 3)],
        }
        for k, steps_of in events.items():
            @pl.when(p == k)
            def _(k=k, steps_of=steps_of):
                for c, stage in steps_of:
                    sum_step(c, stage)
                if k == 2:
                    start_shares(0)
                if k in (2, 4):
                    to_y(1, 1 + k // 2).start()
                if k == 4:
                    for sign in (1, -1):
                        share_step(sign, 1)
        for c in range(1, 4):
            @pl.when(p == 2 * c - 1)
            def _(c=c):
                if c == 3:
                    sum_sent(0)
                for k in range(3):
                    at = pl.ds(k * width + (c - 1) * 256, 256)
                    own_ref[c % 3, :, k * 256 : (k + 1) * 256] = jnp.dot(
                        flipped_ref[...], joint_ref[:, at], preferred_element_type=jnp.float32
                    ).astype(jnp.bfloat16)
                sum_step(c, 0)

        return 0

    lax.fori_loop(0, pairs, attend, 0)

    rounds = [beside_core, beside_x, beside_y]
    rounds += [((plane + 1 - 2 * lax.rem(plane, 2)) * slabs + here, core), (lax.rem(plane + 2, planes) * slabs + here, core)]

    def tally(k):
        return remote(("tally", k), tally_ref.at[2 * k], tally_ref.at[2 * k + 1], rounds[k])

    def tally_step(k):
        tally(k).wait_recv()
        total = tally_ref[2 * k] + tally_ref[2 * k + 1]
        if k + 1 < len(rounds):
            tally_ref[2 * k + 2] = total
            tally(k + 1).start()
        else:
            vector_ref[...] = total

    def finish_step(i, _):
        at = chunk_of(i)
        back = lax.dot_general(joint_ref[at, :], projection_ref[...], NT, preferred_element_type=jnp.float32)
        _, normal, spread_by = row_norm(tokens_ref[at, :].astype(jnp.float32), norms_ref[0:1, :], norms_ref[1:2, :])
        scaled = back * norms_ref[0:1, :]
        inner = (
            scaled
            - jnp.mean(scaled, axis=1, keepdims=True)
            - normal * jnp.mean(scaled * normal, axis=1, keepdims=True)
        )
        token_ref[at, :] += inner * spread_by
        vector_ref[0:1, :] += jnp.sum(back * normal, axis=0, keepdims=True)
        vector_ref[1:2, :] += jnp.sum(back, axis=0, keepdims=True)
        return 0

    def end_made(at, value):
        layer_ref[at, :] = (residual_ref[at, :] + gate_col[at, 0:1] * value).astype(jnp.bfloat16)

    def load(source, into):
        copy = fetch(2, source, into)
        copy.start()
        copy.wait()

    lax.fori_loop(0, steps // 2, finish_step, 0)
    for c, stage in ((0, 6), (1, 4), (2, 2), (3, 1)):
        sum_step(c, stage)
    lax.fori_loop(steps // 2, steps, finish_step, 0)
    tally_ref[0] = vector_ref[...]
    tally(0).start()
    for c, stage in ((0, 7), (1, 5), (2, 3), (3, 2)):
        sum_step(c, stage)
    for piece in range(4):
        to_y(1, piece).wait_send()
    load(made_all.at[0], a_ref)
    for piece in range(2):
        to_core(1, 0, piece).wait_recv()
    load(core_land.at[1, 0], b_ref)
    add_pieces(a_ref, [a_ref, b_ref], rows, 32)
    tally_step(0)
    for c, stage in ((0, 8), (1, 6), (2, 4), (3, 3)):
        sum_step(c, stage)
    for piece in range(4):
        to_y(1, piece).wait_recv()
    load(y_land.at[1], b_ref)
    add_pieces(a_ref, [a_ref, b_ref], rows, 32)
    tally_step(1)
    for c, stage in ((1, 7), (2, 5), (3, 4)):
        sum_step(c, stage)
    unsort(a_ref, end_made)
    tally_step(2)
    for c, stage in ((1, 8), (2, 6), (3, 5)):
        sum_step(c, stage)
    share_end()
    tally_step(3)
    for c, stage in ((2, 7), (3, 6)):
        sum_step(c, stage)
    tally_step(4)
    for c, stage in ((2, 8), (3, 7), (3, 8)):
        sum_step(c, stage)

    for which in range(2):
        for piece in range(2):
            for second in range(2):
                to_core(which, second, piece).wait_send()
    for k in range(3):
        dot_copy(k).wait_send()
    for sign, r in ways:
        @pl.when(target(sign, r)[1])
        def _(sign=sign, r=r):
            share_x(sign, r).wait_send()
    for sign in (1, -1):
        @pl.when(target(sign, 1)[1])
        def _(sign=sign):
            share_z(sign, 1).wait_send()
    for c in (1, 2, 3):
        sum_sent(c)
    for c in range(4):
        for d in range(1, planes):
            sum_copy(c, "zz", d).wait_send()
        for stage in ("second back", "first back", "cc"):
            sum_copy(c, stage).wait_send()
    for k in range(len(rounds)):
        tally(k).wait_send()
    assert len(ids) <= send_sem.shape[0]


def rear_stage(
    tokens, norms, projection, mixing, centroids, route, lengths, cotangent,
    flipped, joint, mixed, logs, residual, place, loads, dots, back, made, near, far, planes, slabs, total_tokens,
):
    count, width = tokens.shape
    rows = back.shape[1]
    half = width // 2
    bf16, f32 = jnp.bfloat16, jnp.float32
    shape = jax.ShapeDtypeStruct
    anywhere = pl.BlockSpec(memory_space=pl.ANY)
    local = pl.BlockSpec(memory_space=pltpu.VMEM)
    dma = pltpu.SemaphoreType.DMA
    packed = near.shape[1:]
    outs = [
        (shape((count, width), bf16), local),
        (shape((count, width), f32), local),
        (shape((16, width), f32), local),
        (shape((width, half), f32), local),
        (shape((half, width), f32), local),
        (shape((4, width, width), bf16), anywhere),
        (shape((2, 2, rows, width), bf16), anywhere),
        (shape((2, rows, width), bf16), anywhere),
        (shape((planes,) + packed, bf16), anywhere),
        (shape((2, planes - 1) + packed, bf16), anywhere),
    ]
    copies = 120
    return pl.pallas_call(
        partial(rear_kernel, planes, slabs, total_tokens),
        out_shape=[o[0] for o in outs],
        in_specs=[pl.BlockSpec(memory_space=pltpu.SMEM)]
        + [local] * 8
        + [anywhere]
        + [local] * 2
        + [anywhere]
        + [local] * 3
        + [anywhere] * 4,
        out_specs=[o[1] for o in outs],
        scratch_shapes=[
            pltpu.VMEM((count, 3 * width), bf16),
            pltpu.VMEM((count, width), f32),
            pltpu.VMEM((count, count), f32),
            pltpu.VMEM((count, width), bf16),
            pltpu.VMEM((rows, width), bf16),
            pltpu.VMEM((rows, width), bf16),
            pltpu.VMEM((count, 8), f32),
            pltpu.VMEM((count, 128), f32),
            pltpu.VMEM((3, 8, rows), f32),
            pltpu.VMEM((2,) + packed, bf16),
            pltpu.VMEM((2,) + packed, bf16),
            pltpu.VMEM((3, width, width), bf16),
            pltpu.VMEM((4, width // 2, width), bf16),
            pltpu.VMEM((4, width // 4, width), bf16),
            pltpu.VMEM((4, width // 8, width), bf16),
            pltpu.VMEM((4, planes - 1, width // 16, half), bf16),
            pltpu.VMEM((4, width // 16, half), bf16),
            pltpu.VMEM((10, 16, width), f32),
            pltpu.VMEM((2, count, 128), f32),
            dma((copies,)),
            dma((copies,)),
            dma((8,)),
        ],
        compiler_params=pltpu.CompilerParams(
            collective_id=1, has_side_effects=True, vmem_limit_bytes=VMEM_LIMIT
        ),
    )(
        lengths[0],
        tokens,
        norms,
        projection,
        mixing,
        centroids,
        route,
        cotangent,
        flipped,
        joint,
        mixed,
        logs,
        residual,
        place,
        loads,
        dots,
        back,
        made,
        near,
        far,
    )


TILE = 256
ALIGN = 16


def aligned_rows(count, experts):
    return -(-(count + experts * (ALIGN - 1)) // ALIGN) * ALIGN


def gelu_pair(values):
    bell = jnp.exp2(values * values * (-0.5 * HALF_LOG))
    near = 1.0 / (1.0 + (0.3275911 * 0.7071067811865476) * jnp.abs(values))
    series = 1.061405429 * 0.5 * near - 1.453152027 * 0.5
    series = series * near + 1.421413741 * 0.5
    series = series * near - 0.284496736 * 0.5
    series = series * near + 0.254829592 * 0.5
    tail = series * near * bell
    below = jnp.where(values >= 0.0, 1.0 - tail, tail)
    return values * below, below + values * bell * 0.3989422804014327


def expert_kernel_body(
    experts,
    sources,
    limit,
    meta_ref,
    sent_all,
    cot_all,
    gate_all,
    up_near,
    up_far,
    down_near,
    down_far,
    back_all,
    made_all,
    dots_all,
    near_out,
    far_out,
    table,
    x_ref,
    c_ref,
    g_ref,
    column_ref,
    up_ref,
    down_ref,
    gu_ref,
    gd_ref,
    pack_ref,
    zero_ref,
    weight_sem,
    in_sem,
    out_sem,
    grad_sem,
    zero_sem,
):
    rows, width = sent_all.shape[1:]
    half = up_near.shape[2]
    own = meta_ref[0]
    spots = sources * experts

    base = 0
    ends = [0] * sources
    for e in range(experts):
        at = base
        for s in range(sources):
            size = meta_ref[1 + s * experts + e]
            table[0, e * sources + s] = size
            table[1, e * sources + s] = ends[s]
            table[2, e * sources + s] = at
            ends[s] = ends[s] + size
            at = at + size
        number = (at - base + (TILE - 1)) // TILE
        table[3, e] = base
        table[4, e] = number
        base = base + number * TILE
    for s in range(sources):
        table[5, s] = ends[s]

    bits = [1 << b for b in range(limit.bit_length()) if ALIGN <= (1 << b)]

    def move(k, act, outward):
        s, e = lax.rem(k, sources), lax.div(k, sources)
        size = table[0, k]
        for piece in bits:
            @pl.when((size & piece) != 0)
            def _(piece=piece):
                offset = size & (piece - 1)
                src = pl.ds(pl.multiple_of(table[1, k] + offset, ALIGN), piece)
                dst = pl.ds(pl.multiple_of(table[2, k] + offset, ALIGN), piece)
                if outward:
                    act(pltpu.make_async_copy(x_ref.at[dst], made_all.at[s, src], out_sem.at[0]))
                    act(pltpu.make_async_copy(c_ref.at[dst], back_all.at[s, src], out_sem.at[1]))
                else:
                    act(pltpu.make_async_copy(sent_all.at[s, src], x_ref.at[dst], in_sem.at[e, 0]))
                    act(pltpu.make_async_copy(cot_all.at[s, src], c_ref.at[dst], in_sem.at[e, 1]))

    def each(low, high, act):
        def one(i, _):
            act(i)
            return 0
        lax.fori_loop(low, high, one, 0)

    def begin(copy):
        copy.start()

    def end(copy):
        copy.wait()

    def move_weights(e, act):
        slot = e - own + experts - 1
        for j, (ups, downs) in enumerate(((up_near, down_near), (up_far, down_far))):
            part = pl.ds(j * half, half)
            act(pltpu.make_async_copy(ups.at[slot], up_ref.at[e, :, part], weight_sem.at[e, j, 0]))
            act(pltpu.make_async_copy(downs.at[slot], down_ref.at[e, part], weight_sem.at[e, j, 1]))

    zero_ref[...] = jnp.zeros_like(zero_ref)

    def bring(e):
        @pl.when(table[4, e] > 0)
        def _():
            last = pl.ds(pl.multiple_of(table[3, e] + (table[4, e] - 1) * TILE, TILE), TILE)
            x_ref[last, :] = jnp.zeros((TILE, width), jnp.bfloat16)
            c_ref[last, :] = jnp.zeros((TILE, width), jnp.bfloat16)
            g_ref[last, :] = jnp.zeros((TILE, 128), jnp.float32)

        move_weights(e, begin)
        each(e * sources, (e + 1) * sources, lambda k: move(k, begin, False))

    each(0, experts, bring)

    chunks = experts + 1

    def tail(k, act):
        s, i = lax.div(k, chunks), lax.rem(k, chunks) + rows // ALIGN - chunks

        @pl.when(i * ALIGN >= table[5, s])
        def _():
            dst = pl.ds(pl.multiple_of(i * ALIGN, ALIGN), ALIGN)
            act(pltpu.make_async_copy(zero_ref, made_all.at[s, dst], zero_sem.at[0]))
            act(pltpu.make_async_copy(zero_ref, back_all.at[s, dst], zero_sem.at[1]))

    each(0, sources * chunks, lambda k: tail(k, begin))

    def shift(s, outward):
        def segment(e):
            k = e * sources + s

            def one(i):
                src = pl.ds(pl.multiple_of(table[1, k] + i * ALIGN, ALIGN), ALIGN)
                dst = pl.ds(pl.multiple_of(table[2, k] + i * ALIGN, ALIGN), ALIGN)
                if outward:
                    column_ref[src, :] = g_ref[dst, :]
                else:
                    g_ref[dst, :] = column_ref[src, :]

            each(0, table[0, k] // ALIGN, one)

        each(0, experts, segment)

    def gates_in(s):
        column_ref[...] = jnp.transpose(jnp.broadcast_to(gate_all[s, 0:1, :], (128, rows)))
        shift(s, False)

    each(0, sources, gates_in)

    def grads(e):
        slot = lax.rem(e, 2)
        return [
            pltpu.make_async_copy(pack_ref.at[slot, j], ref.at[e], grad_sem.at[slot, j])
            for j, ref in enumerate((near_out, far_out))
        ]

    def work(e):
        move_weights(e, end)
        each(e * sources, (e + 1) * sources, lambda k: move(k, end, False))
        gu_ref[...] = jnp.zeros_like(gu_ref)
        gd_ref[...] = jnp.zeros_like(gd_ref)

        def tile(t):
            at = pl.ds(pl.multiple_of(table[3, e] + t * TILE, TILE), TILE)
            x, c, gate = x_ref[at, :], c_ref[at, :], g_ref[at, 0:1]
            before = jnp.dot(x, up_ref[e], preferred_element_type=jnp.float32)
            active, slope = gelu_pair(before)
            through = lax.dot_general(c, down_ref[e], NT, preferred_element_type=jnp.float32)
            grad = (through * (slope * gate)).astype(jnp.bfloat16)
            gated = (active * gate).astype(jnp.bfloat16)
            made = jnp.dot(active.astype(jnp.bfloat16), down_ref[e], preferred_element_type=jnp.float32)
            g_ref[at, :] = jnp.broadcast_to(
                jnp.sum(made * c.astype(jnp.float32), axis=1, keepdims=True), (TILE, 128)
            )
            gd_ref[...] += lax.dot_general(gated, c, TN, preferred_element_type=jnp.float32)
            gu_ref[...] += lax.dot_general(x, grad, TN, preferred_element_type=jnp.float32)
            back = lax.dot_general(grad, up_ref[e], NT, preferred_element_type=jnp.float32)
            x_ref[at, :] = made.astype(jnp.bfloat16)
            c_ref[at, :] = back.astype(jnp.bfloat16)

        each(0, table[4, e], tile)
        each(e * sources, (e + 1) * sources, lambda k: move(k, begin, True))

        @pl.when(e >= 2)
        def _():
            for copy in grads(e - 2):
                copy.wait()

        slot = lax.rem(e, 2)
        for j in range(2):
            pack_ref[slot, j, 0:width, :] = gu_ref[:, j * half : (j + 1) * half].astype(jnp.bfloat16)
            for part in range(2):
                pack_ref[slot, j, width + part * half : width + (part + 1) * half, :] = gd_ref[
                    j * half : (j + 1) * half, part * half : (part + 1) * half
                ].astype(jnp.bfloat16)
        for copy in grads(e):
            copy.start()

    each(0, experts, work)

    def sums_out(s):
        shift(s, True)
        dots_all[s] = jnp.transpose(column_ref[...])[0:8, :]

    each(0, sources, sums_out)
    each(0, spots, lambda k: move(k, end, True))
    each(0, sources * chunks, lambda k: tail(k, end))
    for e in range(max(0, experts - 2), experts):
        for copy in grads(e):
            copy.wait()


def expert_stage(meta, sent, cot, gates, weights, experts, limit):
    sources, rows, width = sent.shape
    half = weights[0].shape[2]
    hidden = 2 * half
    joined = -(-(sources * rows + experts * (TILE - 1)) // TILE) * TILE
    limit = -(-limit // ALIGN) * ALIGN
    anywhere = pl.BlockSpec(memory_space=pl.ANY)
    local = pl.BlockSpec(memory_space=pltpu.VMEM)
    dma = pltpu.SemaphoreType.DMA
    packed = (width + hidden, half)
    return pl.pallas_call(
        partial(expert_kernel_body, experts, sources, limit),
        out_shape=(
            jax.ShapeDtypeStruct((sources, rows, width), jnp.bfloat16),
            jax.ShapeDtypeStruct((sources, rows, width), jnp.bfloat16),
            jax.ShapeDtypeStruct((sources, 8, rows), jnp.float32),
            jax.ShapeDtypeStruct((experts,) + packed, jnp.bfloat16),
            jax.ShapeDtypeStruct((experts,) + packed, jnp.bfloat16),
        ),
        in_specs=[pl.BlockSpec(memory_space=pltpu.SMEM)] + [anywhere] * 2 + [local] + [anywhere] * 4,
        out_specs=(anywhere, anywhere, local, anywhere, anywhere),
        scratch_shapes=[
            pltpu.SMEM((6, sources * experts), jnp.int32),
            pltpu.VMEM((joined, width), jnp.bfloat16),
            pltpu.VMEM((joined, width), jnp.bfloat16),
            pltpu.VMEM((joined, 128), jnp.float32),
            pltpu.VMEM((rows, 128), jnp.float32),
            pltpu.VMEM((experts, width, hidden), jnp.bfloat16),
            pltpu.VMEM((experts, hidden, width), jnp.bfloat16),
            pltpu.VMEM((width, hidden), jnp.float32),
            pltpu.VMEM((hidden, width), jnp.float32),
            pltpu.VMEM((2, 2) + packed, jnp.bfloat16),
            pltpu.VMEM((ALIGN, width), jnp.bfloat16),
            dma((experts, 2, 2)),
            dma((experts, 2)),
            dma((2,)),
            dma((2, 2)),
            dma((2,)),
        ],
        compiler_params=pltpu.CompilerParams(vmem_limit_bytes=VMEM_LIMIT),
        cost_estimate=pl.CostEstimate(
            flops=12 * sources * rows * width * hidden, bytes_accessed=100_000_000, transcendentals=sources * rows * hidden
        ),
    )(meta, sent, cot, gates, *weights)


def arrange(shared, layer, token, vectors, up, down, experts):
    count, width = layer.shape
    third, half = width // 3, width // 2
    steps = 6

    def kernel(shared_ref, layer_ref, token_ref, vectors_ref, up_ref, down_ref, *outs):
        mixing_out, projection_out, layer_out, token_out, up_out, down_out, *vector_outs, centroids_out, balance_out = outs
        mixing_out[...] = shared_ref[0].astype(jnp.float32)
        for k in range(3):
            for c in range(3):
                at = k * width + c * third
                projection_out[:, at : at + third] = shared_ref[1 + c, :, k * third : (k + 1) * third].astype(jnp.float32)
        layer_out[...] = layer_ref[...]
        token_out[...] = token_ref[...]
        up_out[0] = up_ref[...]
        down_out[0] = down_ref[...]
        for i, out in enumerate(vector_outs):
            out[...] = vectors_ref[i]
        centroids_out[...] = vectors_ref[8 : 8 + experts, :]
        balance_out[...] = vectors_ref[4:5, 0:128]

    f32 = jnp.float32
    shape = jax.ShapeDtypeStruct
    rows = lambda n, m: pl.BlockSpec((n // steps, m), lambda i: (i, 0))
    slab = lambda n, m: pl.BlockSpec((1, n // steps, m), lambda i: (0, i, 0))
    whole = lambda *dims: pl.BlockSpec(dims, lambda i: (0,) * len(dims))
    return pl.pallas_call(
        kernel,
        out_shape=[
            shape((width, width), f32),
            shape((width, 3 * width), f32),
            shape((count, width), jnp.bfloat16),
            shape((count, width), f32),
            shape((1, width, half), f32),
            shape((1, half, width), f32),
        ]
        + [shape((width,), f32)] * 4
        + [shape((experts, width), f32), shape((1, 128), f32)],
        grid=(steps,),
        in_specs=[
            pl.BlockSpec((4, width // steps, width), lambda i: (0, i, 0)),
            rows(count, width),
            rows(count, width),
            whole(16, width),
            rows(width, half),
            rows(half, width),
        ],
        out_specs=[
            rows(width, width),
            rows(width, 3 * width),
            rows(count, width),
            rows(count, width),
            slab(width, half),
            slab(half, width),
        ]
        + [whole(width)] * 4
        + [whole(experts, width), whole(1, 128)],
        compiler_params=pltpu.CompilerParams(vmem_limit_bytes=VMEM_LIMIT),
    )(shared, layer, token, vectors, up, down)


def per_device(
    tokens,
    gains,
    shifts,
    projection,
    mixing,
    factors,
    biases,
    centroids,
    expanding,
    contracting,
    routes,
    lengths,
    cotangent,
):
    count, width = tokens.shape
    experts = centroids.shape[0]
    groups = lax.axis_size("expert")
    slabs = groups // experts
    limit = 2 * count // experts
    total_tokens = count * groups * lax.axis_size("tensor")

    norms = jnp.stack((gains, shifts, factors, biases))
    flipped, joint, mixed, logs, residual, place, loads, sent, cot, gates, *weights = front_stage(
        tokens, norms, projection, mixing, centroids, expanding, contracting, routes, lengths, cotangent, experts, slabs
    )
    meta = jnp.concatenate(
        [lax.div(lax.axis_index("expert"), slabs)[None], gates[:, 1, :experts].reshape(-1).astype(jnp.int32)]
    )
    back, made, dots, near, far = expert_stage(meta, sent, cot, gates, weights, experts, limit)
    layer, token, vectors, up, down, shared, *_ = rear_stage(
        tokens, norms, projection, mixing, centroids, routes, lengths, cotangent,
        flipped, joint, mixed, logs, residual, place, loads, dots, back, made, near, far, experts, slabs, total_tokens,
    )
    (
        mixing_grad, projection_grad, layer_output, token_grad, up_grad, down_grad,
        gain_grad, shift_grad, factor_grad, bias_grad, centroid_grad, balance,
    ) = arrange(shared, layer, token, vectors, up, down, experts)
    return (
        layer_output,
        balance[0, 0],
        token_grad,
        gain_grad,
        shift_grad,
        projection_grad,
        mixing_grad,
        factor_grad,
        bias_grad,
        centroid_grad,
        up_grad,
        down_grad,
    )


def solution(mesh):
    placed = (
        P(("expert", "tensor"), None),
        P(),
        P(),
        P(),
        P(),
        P(),
        P(),
        P(),
        P("expert", None, "tensor"),
        P("expert", "tensor", None),
        P(("expert", "tensor"), None),
        P(("expert", "tensor"), None),
        P(("expert", "tensor"), None),
    )
    near = mesh.shape["expert"] == 16 and mesh.shape["tensor"] == 2
    return jax.shard_map(
        per_device if near else moving_tokens,
        mesh=mesh,
        in_specs=placed,
        out_specs=(
            P(("expert", "tensor"), None),
            P(),
            P(("expert", "tensor"), None),
            P(),
            P(),
            P(),
            P(),
            P(),
            P(),
            P(),
            P("expert", None, "tensor"),
            P("expert", "tensor", None),
        ),
        check_vma=False,
    )
```

profile of v0, /device:TPU:0, one launch (start us, length us, event | category | flops | bytes accessed | tf_op | source)
XLA Modules:
  0.0 409.3 jit_solution(7795316899394756670)
XLA Ops:
  0.6 0.7 stack.15
  1.3 0.7 stack.16
  2.0 0.7 stack.17
  2.7 0.7 stack.18
  3.4 0.6 pad_maximum_fusion.norms_ref
  4.0 1.8 copy.26.route_ref
  5.8 116.8 %shard_map.220 = (bf16[768,1152]{1,0:T(8,128)(2,1)}, bf16[1152,2304]{1,0:T(8,128)(2,1)}, bf16[1152,768]{1,0:T(8,128)(2,1)}, f32[6,2,1152]{2,1,0:T(2,128)}, f32[1...) custom-call(s32[4]{0:T(128)} %bitcast.6, ...), custom_call_target="tpu_custom_call" | custom-call | tf_op jit(solution)/shard_map/pallas_call | solution.py:681
  122.5 0.7 convert_reduce_fusion
  123.3 0.1 convert_element_type.7
  123.4 0.6 pad_add_fusion.meta_ref
  124.0 64.2 %shard_map.221 = (bf16[4,1216,768]{2,1,0:T(8,128)(2,1)}, bf16[4,1216,768]{2,1,0:T(8,128)(2,1)}, f32[4,8,1216]{2,1,0:T(8,128)}, bf16[4,1536,384]{2,1,0:T(8,128)(2,1)}, bf16[4,1536,384]{2,1,0:T(8,128)(2,1)}) custom-call(s32[17]{0:T(128)} %pad_add_fusion.meta_ref, bf16[4,1216,768]{2,1,0:T(8,128)(2,1)} %get-tuple-element.57.sent_all, ...), custom_call_target="tpu_custom_call" | custom-call | flops 34426847232 | bytes 100000000 | tf_op jit(solution)/shard_map/pallas_call | solution.py:1648
  188.2 209.8 %shard_map.222 = (bf16[1152,768]{1,0:T(8,128)(2,1)}, f32[1152,768]{1,0:T(8,128)}, f32[16,768]{1,0:T(8,128)}, f32[768,384]{1,0:T(8,128)}, f32[384,768]{1,0:T(8,12...) custom-call(s32[4]{0:T(128)} %bitcast.7, ...), custom_call_target="tpu_custom_call" | custom-call | tf_op jit(solution)/shard_map/pallas_call | solution.py:1349
  398.0 11.1 %shard_map.223 = (f32[768,768]{1,0:T(8,128)}, f32[768,2304]{1,0:T(8,128)}, bf16[1152,768]{1,0:T(8,128)(2,1)}, f32[1152,768]{1,0:T(8,128)}, f32[1,768,384]{2,1,0:...) custom-call(bf16[4,768,768]{2,1,0:T(8,128)(2,1)} %get-tuple-element., ...), custom_call_target="tpu_custom_call" | custom-call | tf_op jit(solution)/shard_map/pallas_call | solution.py:1710
where the time goes:
time: 410 us; the launch traced here: 409 us
  Pallas kernels  402 us (98%)
  local copies, waits for them, and re-layouts  4.6 us (1%)
    pallas_call x1, Pallas kernels, rear_stage(): pl.pallas_call(partial(rear_kernel, planes, slabs, total_tokens), out_sha...  210 us
    pallas_call x1, Pallas kernels, front_stage(): pl.pallas_call(partial(front_kernel, planes, slabs), out_shape=[o[0] for...  117 us
    pallas_call x1, Pallas kernels, expert_stage(): pl.pallas_call(partial(expert_kernel_body, experts, sources, limit), out_...  64.2 us
    pallas_call x1, Pallas kernels, arrange(): pl.pallas_call(kernel, out_shape=[shape((width, width), f32), shape((widt...  11.1 us

commit v1 on v0

--- a/solution.py
+++ b/solution.py
@@ -420,6 +420,17 @@
         at = plane + slot - middle
         return (at >= 0) & (at < planes)
 
+    def handed(kind, sign):
+        i = copies_end + kind
+        return remote(i, fars[kind].at[middle], fars[kind].at[middle - sign], (me + sign * slabs, core))
+
+    def aside_there(slot):
+        if slot == middle - 1:
+            return held(slot) & (plane != 1)
+        if slot == middle + 1:
+            return held(slot) & (plane != planes - 2)
+        return held(slot)
+
     def own_weights(kind):
         return pltpu.make_async_copy(owns[kind].at[0], nears[kind].at[middle], local_sem.at[kind])
 
@@ -436,8 +447,11 @@
             slot = middle - sign * r
 
             @pl.when(hop_came(sign, r))
-            def _(sign=sign, slot=slot):
+            def _(sign=sign):
                 hop(kind, sign, r).wait_recv()
+
+            @pl.when(aside_there(slot))
+            def _(slot=slot):
                 aside(kind, slot).start()
 
             if r < planes - 1:
@@ -446,6 +460,14 @@
                     hop(kind, sign, r + 1).start()
 
     base = 2 * stride
+    copies_end = base + 20
+
+    def hand_on(kind):
+        aside(kind, middle).wait_recv()
+        for sign in (1, -1):
+            @pl.when(plane == (0 if sign > 0 else planes - 1))
+            def _(sign=sign):
+                handed(kind, sign).start()
 
     def row_copy(which, part, piece):
         own, everyone = ((cot_own, cot_all), (sent_own, sent_all))[which]
@@ -555,10 +577,12 @@
         @pl.when(p == 2)
         def _():
             forward_weights(1, 1)
+            hand_on(0)
             tally_step(1)
 
         @pl.when(p == 4)
         def _():
+            hand_on(1)
             forward_weights(0, 2)
             tally_step(2)
 
@@ -644,9 +668,21 @@
                 def _(kind=kind, sign=sign, r=r):
                     hop(kind, sign, r).wait_send()
         for slot in range(2 * planes - 1):
-            @pl.when(held(slot))
+            if slot == middle:
+                aside(kind, slot).wait_send()
+                continue
+
+            @pl.when(aside_there(slot))
             def _(kind=kind, slot=slot):
                 aside(kind, slot).wait()
+        for sign in (1, -1):
+            @pl.when(plane == (0 if sign > 0 else planes - 1))
+            def _(kind=kind, sign=sign):
+                handed(kind, sign).wait_send()
+
+            @pl.when(plane == (1 if sign > 0 else planes - 2))
+            def _(kind=kind, sign=sign):
+                handed(kind, sign).wait_recv()
 
 
 def front_stage(
@@ -661,7 +697,7 @@
     anywhere = pl.BlockSpec(memory_space=pl.ANY)
     local = pl.BlockSpec(memory_space=pltpu.VMEM)
     dma = pltpu.SemaphoreType.DMA
-    copies = 2 * (2 * (planes - 1) + slots) + 12 + 3 + 5
+    copies = 2 * (2 * (planes - 1) + slots) + 12 + 3 + 5 + 2
     outs = [
         (shape((width, count), bf16), local),
         (shape((count, 3 * width), bf16), local),
@@ -757,6 +793,7 @@
     upstream_ref,
     a_ref,
     b_ref,
+    made_ref,
     place_col,
     gate_col,
     dot_land,
@@ -815,9 +852,8 @@
         )
 
     def to_y(which, piece):
-        size = half_rows // (1 + which)
-        at = pl.ds(piece * size, size)
-        return remote(("y", which, piece), a_ref.at[at], y_land.at[which, at], beside_y)
+        at = pl.ds(piece * half_rows, half_rows)
+        return remote(("y", which, piece), (a_ref, made_ref)[which].at[at], y_land.at[which, at], beside_y)
 
     def dot_copy(k):
         return remote(("dot", k), dots_ref.at[1 + k], dot_land.at[k], (beside_core, beside_y, diagonal)[k])
@@ -949,7 +985,7 @@
         return lax.div(p, 2) * q4, pl.multiple_of(lax.rem(p, 2) * half, 128)
 
     def sum_copy(c, stage, d=0):
-        own = own_ref.at[c % 3]
+        own = own_ref.at[c]
         if stage == "core":
             return remote((c, stage), own.at[spot((1 - core) * q1, q1)], own_core.at[c], beside_core)
         if stage == "first":
@@ -980,8 +1016,8 @@
         def one(i, _):
             at = pl.ds(pl.multiple_of(i * step, step), step)
             mine = spot(start + i * step, step)
-            own_ref[c % 3, mine, :] = (
-                own_ref[c % 3, mine, :].astype(jnp.float32) + came[c, at, :].astype(jnp.float32)
+            own_ref[c, mine, :] = (
+                own_ref[c, mine, :].astype(jnp.float32) + came[c, at, :].astype(jnp.float32)
             ).astype(jnp.bfloat16)
             return 0
         lax.fori_loop(0, size // step, one, 0)
@@ -1008,7 +1044,7 @@
                 sum_copy(c, "z", d).start()
         elif stage == 4:
             r, k = corner(plane)
-            total = own_ref[c % 3, spot(base3 + r, q4), pl.ds(k, half)].astype(jnp.float32)
+            total = own_ref[c, spot(base3 + r, q4), pl.ds(k, half)].astype(jnp.float32)
             for d in range(1, planes):
                 sum_copy(c, "z", d).wait_recv()
                 total = total + own_z[c, d - 1].astype(jnp.float32)
@@ -1037,20 +1073,21 @@
             sum_copy(c, "z", d).wait_send()
 
     def sum_for_y(which):
+        into = (a_ref, made_ref)[which]
         for piece in range(2):
             at = pl.ds(piece * half_rows, half_rows)
-            first = fetch(2, alls[which].at[2, at], a_ref.at[at])
+            first = fetch(2, alls[which].at[2, at], into.at[at])
             first.start()
             to_core(which, 1, piece).wait_recv()
             second = fetch(3, core_land.at[which, 1, at], b_ref.at[at])
             second.start()
             first.wait()
             second.wait()
-            add_pieces(a_ref.at[at], [a_ref.at[at], b_ref.at[at]], half_rows, 32)
-            if which == 0:
-                to_y(which, piece).start()
+            add_pieces(into.at[at], [into.at[at], b_ref.at[at]], half_rows, 32)
+            to_y(which, piece).start()
 
     sum_for_y(0)
+    sum_for_y(1)
     place_col[...] = jnp.transpose(place_ref[...])
     score_bias(bias_ref, lengths_ref, count)
     for copy in loads:
@@ -1098,6 +1135,8 @@
     y_back.start()
     y_back.wait()
     unsort(b_ref, add_token)
+    for sign in (1, -1):
+        share_step(sign, planes - 2)
     for k in range(3):
         dot_copy(k).wait_recv()
     dots = dots_ref[0] + dot_land[0] + dot_land[1] + dot_land[2]
@@ -1144,13 +1183,6 @@
         mixed_ref[...], layer_ref[...], TN, preferred_element_type=jnp.float32
     ).astype(jnp.bfloat16)
     sum_step(0, 0)
-    for piece in range(2):
-        to_y(0, piece).wait_send()
-    sum_for_y(1)
-    for piece in range(2):
-        to_y(1, piece).start()
-    for sign in (1, -1):
-        share_step(sign, planes - 2)
 
     first = lax.broadcasted_iota(jnp.int32, (1, 128), 1) < 64
 
@@ -1185,32 +1217,28 @@
         joint_ref[:, values] = value_sum[...].astype(jnp.bfloat16)
 
         events = {
-            0: [(0, 1)],
-            2: [(0, 2), (1, 1)],
-            3: [(0, 3)],
-            4: [(0, 4), (1, 2), (2, 1)],
-            5: [(0, 5), (1, 3)],
+            0: [],
+            1: [(0, 1)],
+            2: [(1, 1)],
+            3: [(0, 2)],
+            4: [(1, 2), (2, 1)],
         }
         for k, steps_of in events.items():
             @pl.when(p == k)
             def _(k=k, steps_of=steps_of):
                 for c, stage in steps_of:
                     sum_step(c, stage)
+                if k == 0:
+                    start_shares(0)
                 if k == 2:
-                    start_shares(0)
-                if k in (2, 4):
-                    to_y(1, 1 + k // 2).start()
-                if k == 4:
                     for sign in (1, -1):
                         share_step(sign, 1)
         for c in range(1, 4):
             @pl.when(p == 2 * c - 1)
             def _(c=c):
-                if c == 3:
-                    sum_sent(0)
                 for k in range(3):
                     at = pl.ds(k * width + (c - 1) * 256, 256)
-                    own_ref[c % 3, :, k * 256 : (k + 1) * 256] = jnp.dot(
+                    own_ref[c, :, k * 256 : (k + 1) * 256] = jnp.dot(
                         flipped_ref[...], joint_ref[:, at], preferred_element_type=jnp.float32
                     ).astype(jnp.bfloat16)
                 sum_step(c, 0)
@@ -1257,47 +1285,47 @@
         copy.start()
         copy.wait()
 
+    def sum_steps(*which):
+        for c, stage in which:
+            sum_step(c, stage)
+
     lax.fori_loop(0, steps // 2, finish_step, 0)
-    for c, stage in ((0, 6), (1, 4), (2, 2), (3, 1)):
-        sum_step(c, stage)
+    sum_steps((3, 1), (0, 3), (1, 3), (2, 2))
     lax.fori_loop(steps // 2, steps, finish_step, 0)
     tally_ref[0] = vector_ref[...]
     tally(0).start()
-    for c, stage in ((0, 7), (1, 5), (2, 3), (3, 2)):
-        sum_step(c, stage)
-    for piece in range(4):
-        to_y(1, piece).wait_send()
+    sum_steps((0, 4), (1, 4), (2, 3))
+    for piece in range(2):
+        to_y(0, piece).wait_send()
     load(made_all.at[0], a_ref)
     for piece in range(2):
         to_core(1, 0, piece).wait_recv()
     load(core_land.at[1, 0], b_ref)
     add_pieces(a_ref, [a_ref, b_ref], rows, 32)
+    sum_steps((3, 2), (0, 5), (1, 5), (2, 4))
     tally_step(0)
-    for c, stage in ((0, 8), (1, 6), (2, 4), (3, 3)):
-        sum_step(c, stage)
-    for piece in range(4):
+    for piece in range(2):
         to_y(1, piece).wait_recv()
     load(y_land.at[1], b_ref)
     add_pieces(a_ref, [a_ref, b_ref], rows, 32)
+    sum_steps((3, 3), (0, 6), (1, 6), (2, 5))
     tally_step(1)
-    for c, stage in ((1, 7), (2, 5), (3, 4)):
-        sum_step(c, stage)
     unsort(a_ref, end_made)
+    sum_steps((3, 4), (2, 6))
     tally_step(2)
-    for c, stage in ((1, 8), (2, 6), (3, 5)):
-        sum_step(c, stage)
     share_end()
+    sum_steps((3, 5), (0, 7), (1, 7))
     tally_step(3)
-    for c, stage in ((2, 7), (3, 6)):
-        sum_step(c, stage)
+    sum_steps((3, 6), (2, 7))
     tally_step(4)
-    for c, stage in ((2, 8), (3, 7), (3, 8)):
-        sum_step(c, stage)
+    sum_steps((0, 8), (1, 8), (2, 8), (3, 7), (3, 8))
 
     for which in range(2):
         for piece in range(2):
             for second in range(2):
                 to_core(which, second, piece).wait_send()
+    for piece in range(2):
+        to_y(1, piece).wait_send()
     for k in range(3):
         dot_copy(k).wait_send()
     for sign, r in ways:
@@ -1308,7 +1336,7 @@
         @pl.when(target(sign, 1)[1])
         def _(sign=sign):
             share_z(sign, 1).wait_send()
-    for c in (1, 2, 3):
+    for c in range(4):
         sum_sent(c)
     for c in range(4):
         for d in range(1, planes):
@@ -1364,12 +1392,13 @@
             pltpu.VMEM((count, width), bf16),
             pltpu.VMEM((rows, width), bf16),
             pltpu.VMEM((rows, width), bf16),
+            pltpu.VMEM((rows, width), bf16),
             pltpu.VMEM((count, 8), f32),
             pltpu.VMEM((count, 128), f32),
             pltpu.VMEM((3, 8, rows), f32),
             pltpu.VMEM((2,) + packed, bf16),
             pltpu.VMEM((2,) + packed, bf16),
-            pltpu.VMEM((3, width, width), bf16),
+            pltpu.VMEM((4, width, width), bf16),
             pltpu.VMEM((4, width // 2, width), bf16),
             pltpu.VMEM((4, width // 4, width), bf16),
             pltpu.VMEM((4, width // 8, width), bf16),

time: 410 us -> 389 us (0.949)
  Pallas kernels: 402 us -> 379 us
    pallas_call x1, Pallas kernels: 210 us -> 189 us  [rear_stage(): pl.pallas_call(partial(rear_kernel, planes, slabs, total_tokens), out_sha...]
where the time goes in v1:
time: 389 us; the launch traced here: 386 us
  Pallas kernels  379 us (97%)
  local copies, waits for them, and re-layouts  4.6 us (1%)
    pallas_call x1, Pallas kernels, rear_stage(): pl.pallas_call(partial(rear_kernel, planes, slabs, total_tokens), out_sha...  189 us
    pallas_call x1, Pallas kernels, front_stage(): pl.pallas_call(partial(front_kernel, planes, slabs), out_shape=[o[0] for...  117 us
    pallas_call x1, Pallas kernels, expert_stage(): pl.pallas_call(partial(expert_kernel_body, experts, sources, limit), out_...  61.8 us
    pallas_call x1, Pallas kernels, arrange(): pl.pallas_call(kernel, out_shape=[shape((width, width), f32), shape((widt...  11.1 us

profile of v1, /device:TPU:0, one launch (start us, length us, event | category | flops | bytes accessed | tf_op | source)
XLA Modules:
  0.0 386.2 jit_solution(11951023289950049860)
XLA Ops:
  0.6 0.7 stack.15
  1.3 0.7 stack.16
  2.0 0.7 stack.17
  2.7 0.7 stack.18
  3.4 0.6 pad_maximum_fusion.norms_ref
  4.0 1.8 copy.26.route_ref
  5.8 116.8 %shard_map.220 = (bf16[768,1152]{1,0:T(8,128)(2,1)}, bf16[1152,2304]{1,0:T(8,128)(2,1)}, bf16[1152,768]{1,0:T(8,128)(2,1)}, f32[6,2,1152]{2,1,0:T(2,128)}, f32[1...) custom-call(s32[4]{0:T(128)} %bitcast.6, ...), custom_call_target="tpu_custom_call" | custom-call | tf_op jit(solution)/shard_map/pallas_call | solution.py:717
  122.6 0.7 convert_reduce_fusion
  123.3 0.1 convert_element_type.7
  123.4 0.6 pad_add_fusion.meta_ref
  124.0 61.8 %shard_map.221 = (bf16[4,1216,768]{2,1,0:T(8,128)(2,1)}, bf16[4,1216,768]{2,1,0:T(8,128)(2,1)}, f32[4,8,1216]{2,1,0:T(8,128)}, bf16[4,1536,384]{2,1,0:T(8,128)(2,1)}, bf16[4,1536,384]{2,1,0:T(8,128)(2,1)}) custom-call(s32[17]{0:T(128)} %pad_add_fusion.meta_ref, bf16[4,1216,768]{2,1,0:T(8,128)(2,1)} %get-tuple-element.57.sent_all, ...), custom_call_target="tpu_custom_call" | custom-call | flops 34426847232 | bytes 100000000 | tf_op jit(solution)/shard_map/pallas_call | solution.py:1677
  185.9 189.0 %shard_map.222 = (bf16[1152,768]{1,0:T(8,128)(2,1)}, f32[1152,768]{1,0:T(8,128)}, f32[16,768]{1,0:T(8,128)}, f32[768,384]{1,0:T(8,128)}, f32[384,768]{1,0:T(8,12...) custom-call(s32[4]{0:T(128)} %bitcast.7, ...), custom_call_target="tpu_custom_call" | custom-call | tf_op jit(solution)/shard_map/pallas_call | solution.py:1377
  374.9 11.1 %shard_map.223 = (f32[768,768]{1,0:T(8,128)}, f32[768,2304]{1,0:T(8,128)}, bf16[1152,768]{1,0:T(8,128)(2,1)}, f32[1152,768]{1,0:T(8,128)}, f32[1,768,384]{2,1,0:...) custom-call(bf16[4,768,768]{2,1,0:T(8,128)(2,1)} %get-tuple-element., ...), custom_call_target="tpu_custom_call" | custom-call | tf_op jit(solution)/shard_map/pallas_call | solution.py:1739

commit v2 on v1

--- a/solution.py
+++ b/solution.py
@@ -331,21 +331,21 @@
     planes,
     slabs,
     lengths_ref,
-    tokens_ref,
+    tokens_in,
     norms_ref,
-    projection_ref,
-    mixing_ref,
+    projection_in,
+    mixing_in,
     centroids_ref,
     route_row_ref,
     route_ref,
-    cot_ref,
+    cot_in,
     up_ref,
     down_ref,
-    flipped_ref,
-    joint_ref,
-    mixed_ref,
+    flipped_out,
+    joint_out,
+    mixed_out,
     logs_ref,
-    residual_ref,
+    residual_out,
     place_ref,
     loads_ref,
     sent_all,
@@ -363,12 +363,26 @@
     cot_own,
     gate_own,
     tally_ref,
+    tokens_ref,
+    projection_ref,
+    mixing_ref,
+    cot_ref,
+    flipped_ref,
+    joint_ref,
+    mixed_ref,
+    residual_ref,
     send_sem,
     recv_sem,
     local_sem,
 ):
     count, width = tokens_ref.shape
     experts = planes
+    pairs_in = ((cot_in, cot_ref), (tokens_in, tokens_ref), (projection_in, projection_ref), (mixing_in, mixing_ref))
+    brought = [pltpu.make_async_copy(a, b, local_sem.at[5 + i]) for i, (a, b) in enumerate(pairs_in)]
+    pairs_out = ((joint_ref, joint_out), (mixed_ref, mixed_out), (residual_ref, residual_out), (flipped_ref, flipped_out))
+    taken = [pltpu.make_async_copy(a, b, local_sem.at[9 + i]) for i, (a, b) in enumerate(pairs_out)]
+    for copy in brought:
+        copy.start()
     rows = sent_own.shape[0]
     half_rows = rows // 2
     pairs = width // 128
@@ -536,6 +550,7 @@
             row_copy(which, 0, piece).start()
             row_copy(which, 1, piece).start()
 
+    brought[0].wait()
     sort_rows(cot_ref, cot_own, 0)
     own_rows(0).start()
 
@@ -547,7 +562,10 @@
         joint_ref[at, :] = jnp.dot(entry, projection_ref[...], preferred_element_type=jnp.float32).astype(jnp.bfloat16)
         return 0
 
+    for copy in brought[1:]:
+        copy.wait()
     lax.fori_loop(0, count // 192, project, 0)
+    taken[0].start()
     score_bias(bias_ref, lengths_ref, count)
     forward_weights(0, 1)
     tally_step(0)
@@ -589,6 +607,7 @@
         return 0
 
     lax.fori_loop(0, pairs, attend, 0)
+    taken[1].start()
 
     lane = lax.broadcasted_iota(jnp.int32, (1, 128), 1)
 
@@ -610,6 +629,7 @@
         return 0
 
     lax.fori_loop(0, count // 192, mix, 0)
+    taken[2].start()
     for piece in range(2):
         at = slice(piece * half_rows, (piece + 1) * half_rows)
         moved = jnp.dot(order_ref[at, :], normed_ref[...], preferred_element_type=jnp.float32)
@@ -635,6 +655,7 @@
     own_rows(2).start()
     for s in range(0, count, 384):
         flipped_ref[:, s : s + 384] = jnp.transpose(entry_ref[s : s + 384, :])
+    taken[3].start()
 
     for kind in range(2):
         forward_weights(kind, 3)
@@ -658,6 +679,8 @@
             gate_copy(part).wait_recv()
     for k in range(len(rounds)):
         tally(k).wait_send()
+    for copy in taken:
+        copy.wait()
     for which in range(3):
         own_rows(which).wait()
     for kind in range(2):
@@ -699,11 +722,11 @@
     dma = pltpu.SemaphoreType.DMA
     copies = 2 * (2 * (planes - 1) + slots) + 12 + 3 + 5 + 2
     outs = [
-        (shape((width, count), bf16), local),
-        (shape((count, 3 * width), bf16), local),
-        (shape((count, width), bf16), local),
+        (shape((width, count), bf16), anywhere),
+        (shape((count, 3 * width), bf16), anywhere),
+        (shape((count, width), bf16), anywhere),
         (shape((pairs, 2, count), f32), local),
-        (shape((count, width), f32), local),
+        (shape((count, width), f32), anywhere),
         (shape((8, count), f32), local),
         (shape((8, 128), f32), local),
         (shape((4, rows, width), bf16), anywhere),
@@ -717,7 +740,7 @@
     return pl.pallas_call(
         partial(front_kernel, planes, slabs),
         out_shape=[o[0] for o in outs],
-        in_specs=[pl.BlockSpec(memory_space=pltpu.SMEM)] + [local] * 8 + [anywhere] * 2,
+        in_specs=[pl.BlockSpec(memory_space=pltpu.SMEM)] + [anywhere, local] + [anywhere] * 2 + [local] * 3 + [anywhere] * 3,
         out_specs=[o[1] for o in outs],
         scratch_shapes=[
             pltpu.VMEM((rows, count), f32),
@@ -728,9 +751,17 @@
             pltpu.VMEM((rows, width), bf16),
             pltpu.VMEM((8, rows), f32),
             pltpu.VMEM((10, 8, 128), f32),
+            pltpu.VMEM(tokens.shape, bf16),
+            pltpu.VMEM(projection.shape, bf16),
+            pltpu.VMEM(mixing.shape, bf16),
+            pltpu.VMEM(cotangent.shape, bf16),
+            pltpu.VMEM((width, count), bf16),
+            pltpu.VMEM((count, 3 * width), bf16),
+            pltpu.VMEM((count, width), bf16),
+            pltpu.VMEM((count, width), f32),
             dma((copies,)),
             dma((copies,)),
-            dma((5,)),
+            dma((13,)),
         ],
         compiler_params=pltpu.CompilerParams(
             collective_id=0, has_side_effects=True, vmem_limit_bytes=VMEM_LIMIT
@@ -758,16 +789,16 @@
     slabs,
     total_tokens,
     lengths_ref,
-    tokens_ref,
+    tokens_in,
     norms_ref,
-    projection_ref,
+    projection_in,
     mixing_ref,
     centroids_ref,
     route_ref,
-    cot_ref,
-    flipped_ref,
+    cot_in,
+    flipped_in,
     joint_in,
-    mixed_ref,
+    mixed_in,
     logs_ref,
     residual_in,
     place_ref,
@@ -777,11 +808,11 @@
     made_all,
     near_all,
     far_all,
-    layer_ref,
-    token_ref,
+    layer_to,
+    token_to,
     vector_ref,
-    up_out,
-    down_out,
+    up_to,
+    down_to,
     shared_out,
     core_land,
     y_land,
@@ -807,6 +838,15 @@
     piece_ref,
     tally_ref,
     key_sums,
+    tokens_ref,
+    projection_ref,
+    cot_ref,
+    flipped_ref,
+    mixed_ref,
+    layer_ref,
+    token_ref,
+    up_out,
+    down_out,
     send_sem,
     recv_sem,
     local_sem,
@@ -827,7 +867,27 @@
     diagonal = (beside_y[0], 1 - core)
     always = plane >= 0
     others = [(lax.rem(plane + d, planes) * slabs + here, core) for d in range(1, planes)]
-    greet([(d, always) for d in [beside_x, beside_y, beside_core, diagonal] + others])
+    across_plane = (me + 3 - 2 * x - 4 * y, core)
+
+    def fetch(i, src, dst):
+        return pltpu.make_async_copy(src, dst, local_sem.at[i])
+
+    loads = [
+        fetch(0, residual_in, residual_ref),
+        fetch(1, joint_in, joint_ref),
+        fetch(8, cot_in, cot_ref),
+        fetch(9, mixed_in, mixed_ref),
+        fetch(10, flipped_in, flipped_ref),
+        fetch(11, tokens_in, tokens_ref),
+        fetch(12, projection_in, projection_ref),
+    ]
+    results = [
+        fetch(13, token_ref, token_to),
+        fetch(14, layer_ref, layer_to),
+        fetch(15, up_out, up_to),
+        fetch(16, down_out, down_to),
+    ]
+    greet([(d, always) for d in [beside_x, beside_y, beside_core, diagonal, across_plane] + others])
     ids = {}
 
     def remote(key, src, dst, device):
@@ -835,13 +895,6 @@
         return pltpu.make_async_remote_copy(
             src_ref=src, dst_ref=dst, send_sem=send_sem.at[i], recv_sem=recv_sem.at[i], device_id=device, device_id_type=MESH
         )
-
-    def fetch(i, src, dst):
-        return pltpu.make_async_copy(src, dst, local_sem.at[i])
-
-    loads = [fetch(0, joint_in, joint_ref), fetch(1, residual_in, residual_ref)]
-    for copy in loads:
-        copy.start()
 
     alls = (back_all, made_all)
 
@@ -988,6 +1041,10 @@
         own = own_ref.at[c]
         if stage == "core":
             return remote((c, stage), own.at[spot((1 - core) * q1, q1)], own_core.at[c], beside_core)
+        if stage == "plane":
+            at = base1 + (y if d == 0 else 1 - y) * q2 + (x if d == 1 else 1 - x) * q3
+            land = own_second.at[c] if d == 2 else own_first.at[c, pl.ds(d * q3, q3)]
+            return remote((c, stage, d), own.at[spot(at, q3)], land, (beside_x, beside_y, across_plane)[d])
         if stage == "first":
             return remote((c, stage), own.at[spot(base1 + (1 - y) * q2, q2)], own_first.at[c], beside_y)
         if stage == "second":
@@ -1003,6 +1060,9 @@
             return remote(
                 (c, stage, d), piece_ref.at[c], out.at[spot(base3 + r, q4), pl.ds(k, half)], others[d - 1]
             )
+        if stage == "plane back":
+            at = spot(base3, q3)
+            return remote((c, stage, d), out.at[at], out.at[at], (beside_x, beside_y, across_plane)[d])
         if stage == "second back":
             at = spot(base3, q3)
             return remote((c, stage), out.at[at], out.at[at], beside_x)
@@ -1066,9 +1126,52 @@
         else:
             sum_copy(c, "cc").wait_recv()
 
+    def last_step(stage):
+        c = 3
+        if stage == 1:
+            sum_copy(c, "core").wait_recv()
+            add_rows(c, base1, q1, own_core, 48)
+            for d in range(3):
+                sum_copy(c, "plane", d).start()
+        elif stage == 2:
+            for d in range(3):
+                sum_copy(c, "plane", d).wait_recv()
+
+            def one(i, _):
+                mine = spot(base3 + i * 48, 48)
+                total = own_ref[c, mine, :].astype(jnp.float32)
+                for d in range(2):
+                    total = total + own_first[c, spot(d * q3 + i * 48, 48), :].astype(jnp.float32)
+                total = total + own_second[c, spot(i * 48, 48), :].astype(jnp.float32)
+                own_ref[c, mine, :] = total.astype(jnp.bfloat16)
+                return 0
+            lax.fori_loop(0, q3 // 48, one, 0)
+            for d in range(1, planes):
+                sum_copy(c, "z", d).start()
+        elif stage == 3:
+            sum_step(c, 4)
+        elif stage == 4:
+            keep_piece(c).wait()
+            for d in range(1, planes):
+                sum_copy(c, "zz", d).wait_recv()
+            for d in range(3):
+                sum_copy(c, "plane back", d).start()
+        elif stage == 5:
+            for d in range(3):
+                sum_copy(c, "plane back", d).wait_recv()
+            sum_copy(c, "cc").start()
+        else:
+            sum_copy(c, "cc").wait_recv()
+
     def sum_sent(c):
-        for stage in ("core", "first", "second"):
-            sum_copy(c, stage).wait_send()
+        sum_copy(c, "core").wait_send()
+        if c < 3:
+            for stage in ("first", "second", "second back", "first back"):
+                sum_copy(c, stage).wait_send()
+        else:
+            for d in range(3):
+                sum_copy(c, "plane", d).wait_send()
+                sum_copy(c, "plane back", d).wait_send()
         for d in range(1, planes):
             sum_copy(c, "z", d).wait_send()
 
@@ -1087,6 +1190,8 @@
             to_y(which, piece).start()
 
     sum_for_y(0)
+    for copy in loads:
+        copy.start()
     sum_for_y(1)
     place_col[...] = jnp.transpose(place_ref[...])
     score_bias(bias_ref, lengths_ref, count)
@@ -1287,11 +1392,15 @@
 
     def sum_steps(*which):
         for c, stage in which:
-            sum_step(c, stage)
+            if c == 3:
+                last_step(stage)
+            else:
+                sum_step(c, stage)
 
     lax.fori_loop(0, steps // 2, finish_step, 0)
     sum_steps((3, 1), (0, 3), (1, 3), (2, 2))
     lax.fori_loop(steps // 2, steps, finish_step, 0)
+    results[0].start()
     tally_ref[0] = vector_ref[...]
     tally(0).start()
     sum_steps((0, 4), (1, 4), (2, 3))
@@ -1311,14 +1420,19 @@
     sum_steps((3, 3), (0, 6), (1, 6), (2, 5))
     tally_step(1)
     unsort(a_ref, end_made)
+    results[1].start()
     sum_steps((3, 4), (2, 6))
     tally_step(2)
     share_end()
+    results[2].start()
+    results[3].start()
     sum_steps((3, 5), (0, 7), (1, 7))
     tally_step(3)
-    sum_steps((3, 6), (2, 7))
+    sum_steps((2, 7),)
     tally_step(4)
-    sum_steps((0, 8), (1, 8), (2, 8), (3, 7), (3, 8))
+    sum_steps((0, 8), (1, 8), (3, 6), (2, 8))
+    for copy in results:
+        copy.wait()
 
     for which in range(2):
         for piece in range(2):
@@ -1341,8 +1455,7 @@
     for c in range(4):
         for d in range(1, planes):
             sum_copy(c, "zz", d).wait_send()
-        for stage in ("second back", "first back", "cc"):
-            sum_copy(c, stage).wait_send()
+        sum_copy(c, "cc").wait_send()
     for k in range(len(rounds)):
         tally(k).wait_send()
     assert len(ids) <= send_sem.shape[0]
@@ -1362,11 +1475,11 @@
     dma = pltpu.SemaphoreType.DMA
     packed = near.shape[1:]
     outs = [
-        (shape((count, width), bf16), local),
-        (shape((count, width), f32), local),
+        (shape((count, width), bf16), anywhere),
+        (shape((count, width), f32), anywhere),
         (shape((16, width), f32), local),
-        (shape((width, half), f32), local),
-        (shape((half, width), f32), local),
+        (shape((width, half), f32), anywhere),
+        (shape((half, width), f32), anywhere),
         (shape((4, width, width), bf16), anywhere),
         (shape((2, 2, rows, width), bf16), anywhere),
         (shape((2, rows, width), bf16), anywhere),
@@ -1378,10 +1491,10 @@
         partial(rear_kernel, planes, slabs, total_tokens),
         out_shape=[o[0] for o in outs],
         in_specs=[pl.BlockSpec(memory_space=pltpu.SMEM)]
-        + [local] * 8
-        + [anywhere]
-        + [local] * 2
-        + [anywhere]
+        + [anywhere, local, anywhere]
+        + [local] * 3
+        + [anywhere] * 4
+        + [local, anywhere]
         + [local] * 3
         + [anywhere] * 4,
         out_specs=[o[1] for o in outs],
@@ -1406,9 +1519,18 @@
             pltpu.VMEM((4, width // 16, half), bf16),
             pltpu.VMEM((10, 16, width), f32),
             pltpu.VMEM((2, count, 128), f32),
+            pltpu.VMEM(tokens.shape, bf16),
+            pltpu.VMEM(projection.shape, bf16),
+            pltpu.VMEM(cotangent.shape, bf16),
+            pltpu.VMEM(flipped.shape, bf16),
+            pltpu.VMEM(mixed.shape, bf16),
+            pltpu.VMEM((count, width), bf16),
+            pltpu.VMEM((count, width), f32),
+            pltpu.VMEM((width, half), f32),
+            pltpu.VMEM((half, width), f32),
             dma((copies,)),
             dma((copies,)),
-            dma((8,)),
+            dma((17,)),
         ],
         compiler_params=pltpu.CompilerParams(
             collective_id=1, has_side_effects=True, vmem_limit_bytes=VMEM_LIMIT

time: 389 us -> 376 us (0.967)
  Pallas kernels: 379 us -> 364 us
    pallas_call x1, Pallas kernels: 189 us -> 181 us  [rear_stage(): pl.pallas_call(partial(rear_kernel, planes, slabs, total_tokens), out_sha...]
    pallas_call x1, Pallas kernels: 117 us -> 110 us  [front_stage(): pl.pallas_call(partial(front_kernel, planes, slabs), out_shape=[o[0] for...]
where the time goes in v2:
time: 376 us; the launch traced here: 372 us
  Pallas kernels  364 us (97%)
  local copies, waits for them, and re-layouts  4.6 us (1%)
    pallas_call x1, Pallas kernels, rear_stage(): pl.pallas_call(partial(rear_kernel, planes, slabs, total_tokens), out_sha...  181 us
    pallas_call x1, Pallas kernels, front_stage(): pl.pallas_call(partial(front_kernel, planes, slabs), out_shape=[o[0] for...  110 us
    pallas_call x1, Pallas kernels, expert_stage(): pl.pallas_call(partial(expert_kernel_body, experts, sources, limit), out_...  61.8 us
    pallas_call x1, Pallas kernels, arrange(): pl.pallas_call(kernel, out_shape=[shape((width, width), f32), shape((widt...  11.1 us

profile of v2, /device:TPU:0, one launch (start us, length us, event | category | flops | bytes accessed | tf_op | source)
XLA Modules:
  0.0 371.9 jit_solution(13256740493997333137)
XLA Ops:
  0.6 0.7 stack.15
  1.3 0.7 stack.16
  2.0 0.7 stack.17
  2.7 0.7 stack.18
  3.4 0.6 pad_maximum_fusion.norms_ref
  4.0 1.8 copy.26.route_ref
  5.8 110.3 %shard_map.220 = (bf16[768,1152]{1,0:T(8,128)(2,1)}, bf16[1152,2304]{1,0:T(8,128)(2,1)}, bf16[1152,768]{1,0:T(8,128)(2,1)}, f32[6,2,1152]{2,1,0:T(2,128)}, f32[1...) custom-call(s32[4]{0:T(128)} %bitcast.6, ...), custom_call_target="tpu_custom_call" | custom-call | tf_op jit(solution)/shard_map/pallas_call | solution.py:740
  116.1 0.7 convert_reduce_fusion
  116.8 0.1 convert_element_type.7
  116.9 0.6 pad_add_fusion.meta_ref
  117.5 61.8 %shard_map.221 = (bf16[4,1216,768]{2,1,0:T(8,128)(2,1)}, bf16[4,1216,768]{2,1,0:T(8,128)(2,1)}, f32[4,8,1216]{2,1,0:T(8,128)}, bf16[4,1536,384]{2,1,0:T(8,128)(2,1)}, bf16[4,1536,384]{2,1,0:T(8,128)(2,1)}) custom-call(s32[17]{0:T(128)} %pad_add_fusion.meta_ref, bf16[4,1216,768]{2,1,0:T(8,128)(2,1)} %get-tuple-element.57.sent_all, ...), custom_call_target="tpu_custom_call" | custom-call | flops 34426847232 | bytes 100000000 | tf_op jit(solution)/shard_map/pallas_call | solution.py:1799
  179.3 181.3 %shard_map.222 = (bf16[1152,768]{1,0:T(8,128)(2,1)}, f32[1152,768]{1,0:T(8,128)}, f32[16,768]{1,0:T(8,128)}, f32[768,384]{1,0:T(8,128)}, f32[384,768]{1,0:T(8,12...) custom-call(s32[4]{0:T(128)} %bitcast.7, ...), custom_call_target="tpu_custom_call" | custom-call | tf_op jit(solution)/shard_map/pallas_call | solution.py:1490
  360.6 11.1 %shard_map.223 = (f32[768,768]{1,0:T(8,128)}, f32[768,2304]{1,0:T(8,128)}, bf16[1152,768]{1,0:T(8,128)(2,1)}, f32[1152,768]{1,0:T(8,128)}, f32[1,768,384]{2,1,0:...) custom-call(bf16[4,768,768]{2,1,0:T(8,128)(2,1)} %get-tuple-element., ...), custom_call_target="tpu_custom_call" | custom-call | tf_op jit(solution)/shard_map/pallas_call | solution.py:1861

commit v3 on v2

--- a/solution.py
+++ b/solution.py
@@ -1126,8 +1126,7 @@
         else:
             sum_copy(c, "cc").wait_recv()
 
-    def last_step(stage):
-        c = 3
+    def last_step(c, stage):
         if stage == 1:
             sum_copy(c, "core").wait_recv()
             add_rows(c, base1, q1, own_core, 48)
@@ -1165,7 +1164,7 @@
 
     def sum_sent(c):
         sum_copy(c, "core").wait_send()
-        if c < 3:
+        if c not in (3,):
             for stage in ("first", "second", "second back", "first back"):
                 sum_copy(c, stage).wait_send()
         else:
@@ -1321,21 +1320,15 @@
         joint_ref[:, keys] = (key_sum[...] * scale).astype(jnp.bfloat16)
         joint_ref[:, values] = value_sum[...].astype(jnp.bfloat16)
 
-        events = {
-            0: [],
-            1: [(0, 1)],
-            2: [(1, 1)],
-            3: [(0, 2)],
-            4: [(1, 2), (2, 1)],
-        }
+        events = {0: [], 1: [(0, 1)], 2: [(1, 1)], 3: [(0, 2)], 4: [(1, 2), (2, 1)], 5: [(0, 3)]}
         for k, steps_of in events.items():
             @pl.when(p == k)
             def _(k=k, steps_of=steps_of):
                 for c, stage in steps_of:
-                    sum_step(c, stage)
+                    (last_step if c in (3,) else sum_step)(c, stage)
                 if k == 0:
                     start_shares(0)
-                if k == 2:
+                if k == 1:
                     for sign in (1, -1):
                         share_step(sign, 1)
         for c in range(1, 4):
@@ -1392,18 +1385,18 @@
 
     def sum_steps(*which):
         for c, stage in which:
-            if c == 3:
-                last_step(stage)
+            if c in (3,):
+                last_step(c, stage)
             else:
                 sum_step(c, stage)
 
     lax.fori_loop(0, steps // 2, finish_step, 0)
-    sum_steps((3, 1), (0, 3), (1, 3), (2, 2))
+    sum_steps((3, 1), (0, 4), (1, 3), (2, 2))
     lax.fori_loop(steps // 2, steps, finish_step, 0)
     results[0].start()
     tally_ref[0] = vector_ref[...]
     tally(0).start()
-    sum_steps((0, 4), (1, 4), (2, 3))
+    sum_steps((0, 5), (1, 4), (2, 3))
     for piece in range(2):
         to_y(0, piece).wait_send()
     load(made_all.at[0], a_ref)
@@ -1411,13 +1404,13 @@
         to_core(1, 0, piece).wait_recv()
     load(core_land.at[1, 0], b_ref)
     add_pieces(a_ref, [a_ref, b_ref], rows, 32)
-    sum_steps((3, 2), (0, 5), (1, 5), (2, 4))
+    sum_steps((3, 2), (0, 6), (1, 5), (2, 4))
     tally_step(0)
     for piece in range(2):
         to_y(1, piece).wait_recv()
     load(y_land.at[1], b_ref)
     add_pieces(a_ref, [a_ref, b_ref], rows, 32)
-    sum_steps((3, 3), (0, 6), (1, 6), (2, 5))
+    sum_steps((3, 3), (0, 7), (1, 6), (2, 5))
     tally_step(1)
     unsort(a_ref, end_made)
     results[1].start()
@@ -1426,7 +1419,7 @@
     share_end()
     results[2].start()
     results[3].start()
-    sum_steps((3, 5), (0, 7), (1, 7))
+    sum_steps((3, 5), (1, 7))
     tally_step(3)
     sum_steps((2, 7),)
     tally_step(4)

time: 376 us -> 368 us (0.979)
  Pallas kernels: 364 us -> 357 us
    pallas_call x1, Pallas kernels: 181 us -> 174 us  [rear_stage(): pl.pallas_call(partial(rear_kernel, planes, slabs, total_tokens), out_sha...]
where the time goes in v3:
time: 368 us; the launch traced here: 365 us
  Pallas kernels  357 us (97%)
  local copies, waits for them, and re-layouts  4.6 us (1%)
    pallas_call x1, Pallas kernels, rear_stage(): pl.pallas_call(partial(rear_kernel, planes, slabs, total_tokens), out_sha...  174 us
    pallas_call x1, Pallas kernels, front_stage(): pl.pallas_call(partial(front_kernel, planes, slabs), out_shape=[o[0] for...  110 us
    pallas_call x1, Pallas kernels, expert_stage(): pl.pallas_call(partial(expert_kernel_body, experts, sources, limit), out_...  61.8 us
    pallas_call x1, Pallas kernels, arrange(): pl.pallas_call(kernel, out_shape=[shape((width, width), f32), shape((widt...  11.1 us

profile of v3, /device:TPU:0, one launch (start us, length us, event | category | flops | bytes accessed | tf_op | source)
XLA Modules:
  0.0 364.6 jit_solution(3968326170404779512)
XLA Ops:
  0.6 0.7 stack.15
  1.3 0.7 stack.16
  2.0 0.7 stack.17
  2.7 0.7 stack.18
  3.4 0.6 pad_maximum_fusion.norms_ref
  4.0 1.8 copy.26.route_ref
  5.8 110.3 %shard_map.220 = (bf16[768,1152]{1,0:T(8,128)(2,1)}, bf16[1152,2304]{1,0:T(8,128)(2,1)}, bf16[1152,768]{1,0:T(8,128)(2,1)}, f32[6,2,1152]{2,1,0:T(2,128)}, f32[1...) custom-call(s32[4]{0:T(128)} %bitcast.6, ...), custom_call_target="tpu_custom_call" | custom-call | tf_op jit(solution)/shard_map/pallas_call | solution.py:740
  116.1 0.7 convert_reduce_fusion
  116.8 0.1 convert_element_type.7
  116.9 0.6 pad_add_fusion.meta_ref
  117.5 61.8 %shard_map.221 = (bf16[4,1216,768]{2,1,0:T(8,128)(2,1)}, bf16[4,1216,768]{2,1,0:T(8,128)(2,1)}, f32[4,8,1216]{2,1,0:T(8,128)}, bf16[4,1536,384]{2,1,0:T(8,128)(2,1)}, bf16[4,1536,384]{2,1,0:T(8,128)(2,1)}) custom-call(s32[17]{0:T(128)} %pad_add_fusion.meta_ref, bf16[4,1216,768]{2,1,0:T(8,128)(2,1)} %get-tuple-element.57.sent_all, ...), custom_call_target="tpu_custom_call" | custom-call | flops 34426847232 | bytes 100000000 | tf_op jit(solution)/shard_map/pallas_call | solution.py:1792
  179.3 174.0 %shard_map.222 = (bf16[1152,768]{1,0:T(8,128)(2,1)}, f32[1152,768]{1,0:T(8,128)}, f32[16,768]{1,0:T(8,128)}, f32[768,384]{1,0:T(8,128)}, f32[384,768]{1,0:T(8,12...) custom-call(s32[4]{0:T(128)} %bitcast.7, ...), custom_call_target="tpu_custom_call" | custom-call | tf_op jit(solution)/shard_map/pallas_call | solution.py:1483
  353.3 11.1 %shard_map.223 = (f32[768,768]{1,0:T(8,128)}, f32[768,2304]{1,0:T(8,128)}, bf16[1152,768]{1,0:T(8,128)(2,1)}, f32[1152,768]{1,0:T(8,128)}, f32[1,768,384]{2,1,0:...) custom-call(bf16[4,768,768]{2,1,0:T(8,128)(2,1)} %get-tuple-element., ...), custom_call_target="tpu_custom_call" | custom-call | tf_op jit(solution)/shard_map/pallas_call | solution.py:1854
